TPU v7x, 256 devices: a whole 4x4x8 slice. The times are simulated.
256 devices in a mesh: seg: 64 (over z_hi, x, y, core), det: 4 (over z_lo).
Axes of the slice: x: 4, y: 4, z: 8 (z_hi: 2, z_lo: 4; z = z_hi * 4 + z_lo), core: 2. Of those that a mesh axis runs over, the one named last changes fastest.
Arguments:
- strain: float32 [196608, 1024], P('seg', 'det'), may hold values from -6 to 6
- row_target: int32 [196608], P('seg'), may hold values from -1 to 98303, as said below
- gate_start: int32 [64, 3], P('seg'), may hold values from 0 to 458752
- gate_width: int32 [64, 3], P('seg'), may hold values from 8192 to 65536
- inverse_psd: float32 [3, 512, 512], P(None, 'det'), may hold values from 0.2 to 2
- templates: bfloat16 [256, 512, 2, 512], P('seg', 'det'), may hold values from -6 to 6
- template_shift: int32 [256], P('seg'), may hold values from 0 to 1023
Outputs:
- snr: bfloat16 [64, 4, 3, 256, 2, 1024], P('seg', 'det')
Inputs may be any that keep to these rules, and one draw needn't show every extreme that they name: `row_target`: each segment row s * 3 * 512 + r with 0 <= r < 1536 stands in exactly one slot and every other slot holds -1. A reader holds equally many rows of every segment, at most 48, and some reader holds exactly 48 rows of each segment.
All inputs are finite; a program needn't handle non-finite values.
Results may differ from a plain program's by a relative error of at most 0.011.
Values may be sent and summed in bfloat16 or wider, within the bound.
A program may use at most 128 MiB of HBM per device.

v0:
```python
import math

import jax
import jax.numpy as jnp
from jax import lax
from jax.sharding import PartitionSpec as P

V = 512
U = 1024
DETECTORS = 3
BLOCK = 4
STEPS = 3
SAMPLES = 524288


def passed_along(value, axis, steps):
    count = lax.axis_size(axis)
    pairs = [(source, (source + steps) % count) for source in range(count)]
    return lax.ppermute(value, axis, pairs)


def phases(row_index, col_index, modulus, direction):
    residue = row_index[:, None] * col_index[None, :] % modulus
    phase_angle = direction * 2.0 * math.pi / modulus * residue.astype(jnp.float32)
    return (jnp.cos(phase_angle), jnp.sin(phase_angle))


def rotate(real_part, imag_part, cosine, sine_value):
    return (
        real_part * cosine - imag_part * sine_value,
        real_part * sine_value + imag_part * cosine,
    )


def rotation_table(row_index, col_index, modulus, direction, scaling):
    cosine, sine_value = phases(row_index, col_index, modulus, direction)
    upper_rows = jnp.concatenate([cosine, sine_value], axis=1)
    lower_rows = jnp.concatenate([-sine_value, cosine], axis=1)
    return (jnp.concatenate([upper_rows, lower_rows], axis=0) * scaling).astype(jnp.bfloat16)


def row_transform(depth, direction):
    depth_index = jnp.arange(depth, dtype=jnp.int32)
    cosine, sine_value = phases(depth_index, depth_index, depth, direction)
    return (jnp.stack([cosine, sine_value], axis=1) / math.sqrt(depth)).astype(jnp.bfloat16)


def output_table(depth):
    middle_rows = jnp.arange(depth // 4, 3 * depth // 4, dtype=jnp.int32)
    cosine, sine_value = phases(middle_rows, jnp.arange(depth, dtype=jnp.int32), depth, 1.0)
    table = jnp.stack(
        [jnp.stack([cosine, -sine_value], axis=1), jnp.stack([sine_value, cosine], axis=1)], axis=1
    )
    return (table / math.sqrt(depth)).astype(jnp.bfloat16)


def shift_template(template, shift_value, bin_index):
    residue = bin_index * shift_value % SAMPLES
    phase_angle = -2.0 * math.pi / SAMPLES * residue.astype(jnp.float32)
    real_part, imag_part = rotate(
        template[:, 0].astype(jnp.float32),
        template[:, 1].astype(jnp.float32),
        jnp.cos(phase_angle),
        jnp.sin(phase_angle),
    )
    return jnp.stack([real_part, imag_part], axis=1).astype(jnp.bfloat16)


def correlate(coherent, template):
    real_part = coherent[:, 0] * template[..., 0, :] + coherent[:, 1] * template[..., 1, :]
    imag_part = coherent[:, 1] * template[..., 0, :] - coherent[:, 0] * template[..., 1, :]
    return jnp.stack([real_part, imag_part], axis=-2).astype(jnp.bfloat16)


def body(strain, row_target, gate_start, gate_width, inverse_psd, templates, template_shift):
    seg_count = lax.axis_size("seg")
    det_count = lax.axis_size("det")
    det_rank = lax.axis_index("det")
    slot_count, quarter = strain.shape
    seg_rows = DETECTORS * V
    capacity = slot_count // seg_count
    owner_index = jnp.where(row_target >= 0, row_target // seg_rows, seg_count)
    onehot = (owner_index[:, None] == jnp.arange(seg_count, dtype=jnp.int32)[None, :]).astype(
        jnp.int32
    )
    ranking = jnp.sum(jnp.cumsum(onehot, axis=0) * onehot, axis=1) - 1
    destination = jnp.where(row_target >= 0, owner_index * capacity + ranking, slot_count)
    source = (
        jnp.full((slot_count + 1,), slot_count, jnp.int32)
        .at[destination]
        .set(jnp.arange(slot_count, dtype=jnp.int32))[:slot_count]
    )
    padded_rows = jnp.concatenate([strain, jnp.zeros((1, quarter), jnp.float32)], axis=0)
    padded_target = jnp.concatenate([row_target, jnp.full((1,), -1, jnp.int32)])
    chosen = padded_target[source]
    send_rows = padded_rows[source].reshape(seg_count, capacity, quarter)
    send_index = jnp.where(chosen >= 0, chosen % seg_rows, seg_rows).reshape(seg_count, capacity)
    arrived_rows, arrived_index = (
        lax.all_to_all(
            send_rows.astype(jnp.bfloat16), "seg", split_axis=0, concat_axis=0, tiled=True
        ).astype(send_rows.dtype),
        lax.all_to_all(send_index, "seg", split_axis=0, concat_axis=0, tiled=True),
    )
    segment_rows = (
        jnp.zeros((seg_rows + 1, quarter), jnp.float32)
        .at[arrived_index.reshape(-1)]
        .set(arrived_rows.reshape(-1, quarter))[:seg_rows]
    )
    segment_rows = segment_rows.reshape(DETECTORS, V, quarter)
    depth_index = jnp.arange(V, dtype=jnp.int32)
    column = det_rank * quarter + jnp.arange(quarter, dtype=jnp.int32)
    sample_index = depth_index[:, None] * U + column[None, :]
    gate_begin = gate_start[0][:, None, None]
    gate_end = gate_begin + gate_width[0][:, None, None]
    inside = (sample_index[None] >= gate_begin) & (sample_index[None] < gate_end)
    gated_rows = jnp.where(inside, 0.0, segment_rows).astype(jnp.bfloat16)
    first_section = jnp.einsum(
        "krv,dvu->dkru", row_transform(V, -1.0), gated_rows, preferred_element_type=jnp.float32
    )
    twist_cos, twist_sin = phases(depth_index, column, SAMPLES, -1.0)
    real_first, imag_first = rotate(
        first_section[:, :, 0], first_section[:, :, 1], twist_cos, twist_sin
    )
    turned = jnp.stack([real_first, imag_first], axis=2).astype(jnp.bfloat16)
    swapped = lax.all_to_all(turned, "det", split_axis=1, concat_axis=3, tiled=True)
    depth_local = V // det_count
    half_columns = jnp.arange(U // 2, dtype=jnp.int32)
    full_columns = jnp.arange(U, dtype=jnp.int32)
    forward_columns = rotation_table(full_columns, half_columns, U, -1.0, 1.0 / math.sqrt(U))
    spectrum = jnp.dot(
        swapped.reshape(DETECTORS * depth_local, 2 * U),
        forward_columns,
        preferred_element_type=jnp.float32,
    ).reshape(DETECTORS, depth_local, 2, U // 2)
    coherent = jnp.sum(inverse_psd[:, :, None, :] * spectrum, axis=0)
    local_depth = det_rank * depth_local + jnp.arange(depth_local, dtype=jnp.int32)
    bin_index = local_depth[:, None] + V * half_columns[None, :]
    shifted = jax.vmap(shift_template, in_axes=(0, 0, None))(templates, template_shift, bin_index)
    block_list = [shifted]
    moving = shifted
    for cycle_step in range(1, STEPS):
        moving = passed_along(moving, "seg", -1)
        block_list.append(moving)
    inverse_columns = rotation_table(half_columns, full_columns, U, 1.0, 1.0 / math.sqrt(U))
    last_rows = output_table(V)
    results = []
    for template_block in block_list:
        product = correlate(coherent, template_block)
        back_cos, back_sin = phases(local_depth, full_columns, SAMPLES, 1.0)
        series = jnp.dot(
            product.reshape(BLOCK * depth_local, U),
            inverse_columns,
            preferred_element_type=jnp.float32,
        ).reshape(BLOCK, depth_local, 2, U)
        real_back, imag_back = rotate(series[:, :, 0], series[:, :, 1], back_cos, back_sin)
        turned_back = jnp.stack([real_back, imag_back], axis=2).astype(jnp.bfloat16)
        partial_value = jnp.einsum(
            "vpqk,tkqu->tvpu",
            last_rows,
            lax.all_to_all(turned_back, "det", split_axis=3, concat_axis=1, tiled=True),
            preferred_element_type=jnp.float32,
        ).astype(jnp.bfloat16)
        result = lax.all_to_all(partial_value, "det", split_axis=0, concat_axis=3, tiled=True)
        results.append(result)
    return jnp.stack(results, axis=1)[None]


def solution(mesh):
    in_specs = (
        P("seg", "det"),
        P("seg"),
        P("seg", None),
        P("seg", None),
        P(None, "det", None),
        P("seg", "det", None, None),
        P("seg"),
    )
    out_specs = P("seg", "det", None, None, None, None)
    return jax.shard_map(body, mesh=mesh, in_specs=in_specs, out_specs=out_specs, check_vma=False)
```

profile of v0, /device:TPU:1, one launch (start us, length us, event | category | flops | bytes accessed | tf_op | source)
XLA Modules:
  0.0 545.6 jit_solution(6689443895357056759)
XLA Ops:
  0.8 18.3 %reduce-window.6 = s32[64,24,128]{2,1,0:T(8,128)S(1)} reduce-window(s32[64,24,128]{2,1,0:T(8,128)S(1)} %fusion.87, s32[]{:T(128)} %constant.135.clone.1), window={size=1x1x128 pad=0_0x0_0x127_0}, to_apply=%region_0.1 | reduce-window | flops 24969216 | bytes 1572868 | tf_op jit(solution)/shard_map/reduce-window
  20.5 11.8 %scatter_custom_fusion = s32[3073]{0:T(1024)S(1)} fusion(s32[3072]{0:T(1024)S(1)} %compare_select_fusion.2, s32[3072]{0:T(1024)S(1)} %iota.96, s32[]{:T(128)} %constant.134.clone.1), kind=kCustom, calls=%fused_computation.197 | custom fusion | bytes 12296 | tf_op jit(solution)/shard_map/scatter | solution.py:91
  32.4 17.4 %gather_fusion = s32[3072]{0:T(1024)S(1)} fusion(s32[3073]{0:T(1024)S(1)} %pad_add_fusion, s32[3072]{0:T(1024)S(1)} %fusion.119), kind=kCustom, calls=%fused_computation | custom fusion | bytes 36864 | tf_op jit(solution)/shard_map/gather | solution.py:95
  50.6 15.6 %all-to-all-start = ((s32[64,1,48]{2,1,0:T(1,128)}), s32[64,1,48]{2,1,0:T(1,128)S(1)}, u32[]{:S(2)}, u32[]{:S(2)}) async-start(s32[64,1,48]{2,1,0:T(1,128)} %bitcast.6), calls=%async_computation | async-start | bytes 65536 | tf_op jit(solution)/shard_map/all_to_all | solution.py:102
  66.2 2.0 concatenate.25
  68.3 13.0 %gather_fusion.1 = bf16[3072,256]{1,0:T(8,128)(2,1)} fusion(bf16[3073,256]{1,0:T(8,128)(2,1)S(1)} %concatenate.25, s32[3072]{0:T(1024)S(1)} %fusion.119), kind=kCustom, calls=%fused_computation.1 | custom fusion | bytes 3158016 | tf_op jit(solution)/shard_map/gather | solution.py:96
  81.3 12.8 %all-to-all-start.1 = ((bf16[64,48,256]{2,1,0:T(8,128)(2,1)}), bf16[64,48,256]{2,1,0:T(8,128)(2,1)S(1)}, u32[]{:S(2)}, u32[]{:S(2)}) async-start(bf16[64,48,256]{2,1,0:T(8,128)(2,1)} %bitcast.8), calls=%async_computation.1 | async-start | bytes 3145728 | tf_op jit(solution)/shard_map/all_to_all | solution.py:99
  95.3 5.0 fusion.105
  100.3 3.2 fusion.115
  104.9 20.1 %all-to-all-done.1 = bf16[64,48,256]{2,1,0:T(8,128)(2,1)S(1)} async-done(((bf16[64,48,256]{2,1,0:T(8,128)(2,1)}), bf16[64,48,256]{2,1,0:T(8,128)(2,1)S(1)}, u32[]{:S(2)}, u32[]{:S(2)}) %all-to-all-start.1) | async-done | bytes 1572896 | tf_op jit(solution)/shard_map/all_to_all | solution.py:99
  124.9 13.7 %scatter_custom_fusion.1 = f32[1537,256]{1,0:T(8,128)S(1)} fusion(s32[3072]{0:T(1024)S(1)} %bitcast.189, bf16[3072,256]{1,0:T(8,128)(2,1)S(1)} %bitcast.172, f32[]{:T(128)} %constant.132.clone.1), kind=kCustom, calls=%fused_computation.9 | custom fusion | flops 786432 | bytes 3146756 | tf_op jit(solution)/shard_map/scatter | solution.py:107
  138.8 3.0 convolution_bitcast_fusion
  142.6 3.0 copy.65
  145.6 14.7 %all-to-all-start.2 = ((bf16[3,512,2,256]{3,2,0,1:T(2,128)(2,1)}), bf16[3,512,2,256]{3,2,0,1:T(2,128)(2,1)}, u32[]{:S(2)}, u32[]{:S(2)}) async-start(bf16[3,512,2,256]{3,2,0,1:T(2,128)(2,1)} %copy.65), calls=%async_computation.2 | async-start | bytes 3145728 | tf_op jit(solution)/shard_map/all_to_all | solution.py:125
  160.4 9.0 %fusion.70 = (f32[1024,512]{0,1:T(8,128)S(1)}, f32[1024,512]{0,1:T(8,128)}) fusion(), kind=kLoop, calls=%fused_computation.122 | loop fusion | flops 7340032 | bytes 4194304 | tf_op jit(solution)/shard_map/sin | solution.py:25
  169.4 8.6 %fusion.76 = f32[1024,512]{0,1:T(8,128)} fusion(), kind=kLoop, calls=%fused_computation.128 | loop fusion | flops 7864320 | bytes 2097152 | tf_op jit(solution)/shard_map/neg | solution.py:38
  178.7 2.4 fusion.132
  181.2 6.4 %fusion = bf16[2048,1024]{0,1:T(8,128)(2,1)} fusion(f32[1024,512]{0,1:T(8,128)} %get-tuple-element.43, f32[1024,512]{0,1:T(8,128)} %fusion.76, f32[1024,512]{0,1:T(8,128)S(1)} %get-tuple-element.42), kind=kLoop, calls=%fused_computation.5 | loop fusion | flops 10485760 | bytes 10485760 | tf_op jit(solution)/shard_map/convert_element_type | solution.py:39
  187.6 10.7 %all-to-all-done.2 = bf16[3,512,2,256]{3,2,0,1:T(2,128)(2,1)} async-done(((bf16[3,512,2,256]{3,2,0,1:T(2,128)(2,1)}), bf16[3,512,2,256]{3,2,0,1:T(2,128)(2,1)}, u32[]{:S(2)}, u32[]{:S(2)}) %all-to-all-start.2) | async-done | bytes 1572896 | tf_op jit(solution)/shard_map/all_to_all | solution.py:125
  198.3 3.4 copy.124
  203.0 4.4 multiply_reduce_fusion
  207.5 5.6 %fusion.48 = (bf16[4,128,1,512]{3,1,2,0:T(8,128)(2,1)}, bf16[4,128,1,512]{3,1,2,0:T(8,128)(2,1)S(1)}, bf16[4,128,1,512]{3,1,2,0:T(8,128)(2,1)S(1)}) fusion(f32[128,512]{1,0:T(8,128)S(1)} %get-tuple-element.32, f32[128,512]{1,0:T(8,128)S(1)} %get-tuple-element.31, bf16[4,128,1,512]{3,2,1,0:T(2,128)(2,1)S(1)} %copy-done.7, s32[4]{0:T(128)S(1)} %copy-done.21, ...), kind=kLoop, calls=%fused_computation.95 | loop fusion | flops 7864320 | bytes 3407888 | tf_op jit(solution)/shard_map/convert.11
  214.0 13.6 %collective-permute-done = bf16[4,128,2,512]{3,1,2,0:T(8,128)(2,1)} collective-permute-done((bf16[4,128,2,512]{3,1,2,0:T(8,128)(2,1)S(1)}, bf16[4,128,2,512]{3,1,2,0:T(8,128)(2,1)}, u32[]{:S(2)}, u32[]{:S(2)}) %collective-permute-start) | collective-permute-done | bytes 1048608 | tf_op jit(solution)/shard_map/ppermute | solution.py:19
  227.6 11.6 %collective-permute-start.1 = (bf16[4,128,2,512]{3,1,2,0:T(8,128)(2,1)}, bf16[4,128,2,512]{3,1,2,0:T(8,128)(2,1)}, u32[]{:S(2)}, u32[]{:S(2)}) collective-permute-start(bf16[4,128,2,512]{3,1,2,0:T(8,128)(2,1)} %collective-permute-done), channel_id=1, source_target_pairs={{0,252},{4,0},{8,4},{12,8},{16,12},{20,16},{24,20},{28,24},{32,28}... | collective-permute-start | bytes 3145736 | tf_op jit(solution)/shard_map/ppermute | solution.py:19
  239.2 9.0 %fusion.68 = (f32[512,1024]{0,1:T(8,128)S(1)}, f32[512,1024]{0,1:T(8,128)}) fusion(), kind=kLoop, calls=%fused_computation.120 | loop fusion | flops 7340032 | bytes 4194304 | tf_op jit(solution)/shard_map/sin | solution.py:25
  248.2 8.6 %fusion.77 = f32[512,1024]{0,1:T(8,128)} fusion(), kind=kLoop, calls=%fused_computation.129 | loop fusion | flops 7864320 | bytes 2097152 | tf_op jit(solution)/shard_map/neg | solution.py:38
  256.7 3.2 fusion.113
  259.9 6.5 %fusion.1 = bf16[1024,2048]{0,1:T(8,128)(2,1)} fusion(f32[512,1024]{0,1:T(8,128)} %get-tuple-element.47, f32[512,1024]{0,1:T(8,128)} %fusion.77, f32[512,1024]{0,1:T(8,128)S(1)} %get-tuple-element.46), kind=kLoop, calls=%fused_computation.7 | loop fusion | flops 10485760 | bytes 10485760 | tf_op jit(solution)/shard_map/convert_element_type | solution.py:39
  266.5 3.2 fusion.52
  272.6 6.7 %fusion.135 = f32[4,128,2,1024]{3,1,2,0:T(8,128)} fusion(bf16[4,128,1024,1]{1,2,3,0:T(8,128)(2,1)S(1)} %bitcast.183, bf16[2,1024,1024,1]{2,1,0,3:T(8,128)(2,1)} %bitcast.173), kind=kOutput, calls=%fused_computation.215 | convolution fusion | flops 2147483648 | bytes 9437184 | tf_op jit(solution)/shard_map/dot_general | solution.py:150
  279.3 4.4 fusion.134
  284.8 4.7 fusion.133
  289.6 3.4 subtract_convert_fusion.2
  293.3 4.0 copy.71
  297.3 3.6 all-to-all-start.3
  300.9 3.1 pad_maximum_fusion.1
  304.0 6.2 %copy.76 = bf16[4,128,2,1024]{1,2,0,3:T(2,128)(2,1)} copy(bf16[4,128,2,1024]{3,1,2,0:T(8,128)(2,1)} %pad_maximum_fusion.1) | data formatting | bytes 4194304 | tf_op jit(solution)/shard_map/stack | solution.py:156
  310.1 34.4 %all-to-all-done.3 = bf16[4,128,2,1024]{1,2,0,3:T(2,128)(2,1)S(1)} async-done(((bf16[4,128,2,1024]{1,2,0,3:T(2,128)(2,1)}), bf16[4,128,2,1024]{1,2,0,3:T(2,128)(2,1)S(1)}, u32[]{:S(2)}, u32[]{:S(2)}) %all-to-all-start.3) | async-done | bytes 2097184 | tf_op jit(solution)/shard_map/all_to_all | solution.py:160
  344.5 1.4 copy-done
  345.9 3.6 all-to-all-start.5
  349.5 2.7 pad_maximum_fusion.2
  352.3 6.2 %copy.81 = bf16[4,128,2,1024]{1,2,0,3:T(2,128)(2,1)} copy(bf16[4,128,2,1024]{3,1,2,0:T(8,128)(2,1)} %pad_maximum_fusion.2) | data formatting | bytes 4194304 | tf_op jit(solution)/shard_map/stack | solution.py:156
  358.4 38.7 %all-to-all-done.5 = bf16[4,128,2,1024]{1,2,0,3:T(2,128)(2,1)S(1)} async-done(((bf16[4,128,2,1024]{1,2,0,3:T(2,128)(2,1)}), bf16[4,128,2,1024]{1,2,0,3:T(2,128)(2,1)S(1)}, u32[]{:S(2)}, u32[]{:S(2)}) %all-to-all-start.5) | async-done | bytes 2097184 | tf_op jit(solution)/shard_map/all_to_all | solution.py:160
  397.2 4.4 all-to-all-start.7
  401.6 2.1 fusion.116
  405.8 2.9 copy.123
  408.7 4.1 reshape.628
  412.8 4.1 fusion.34
  417.0 32.4 %all-to-all-done.7 = bf16[4,128,2,1024]{1,2,0,3:T(2,128)(2,1)} async-done(((bf16[4,128,2,1024]{1,2,0,3:T(2,128)(2,1)}), bf16[4,128,2,1024]{1,2,0,3:T(2,128)(2,1)}, u32[]{:S(2)}, u32[]{:S(2)}) %all-to-all-start.7) | async-done | bytes 2097184 | tf_op jit(solution)/shard_map/all_to_all | solution.py:160
  449.4 3.8 all-to-all-start.4
  453.2 2.9 copy.122
  456.1 2.7 reshape.632
  458.8 3.8 fusion.37
  462.7 15.7 %all-to-all-done.4 = bf16[4,256,2,256]{1,3,2,0:T(8,128)(2,1)S(1)} async-done(((bf16[4,256,2,256]{1,3,2,0:T(8,128)(2,1)}), bf16[4,256,2,256]{1,3,2,0:T(8,128)(2,1)S(1)}, u32[]{:S(2)}, u32[]{:S(2)}) %all-to-all-start.4) | async-done | bytes 1048608 | tf_op jit(solution)/shard_map/all_to_all | solution.py:163
  478.3 4.2 all-to-all-start.6
  482.6 3.2 copy.121
  485.8 2.2 reshape.635
  488.0 4.4 fusion.40
  492.5 15.4 %all-to-all-done.6 = bf16[4,256,2,256]{1,3,2,0:T(8,128)(2,1)} async-done(((bf16[4,256,2,256]{1,3,2,0:T(8,128)(2,1)}), bf16[4,256,2,256]{1,3,2,0:T(8,128)(2,1)}, u32[]{:S(2)}, u32[]{:S(2)}) %all-to-all-start.6) | async-done | bytes 1048608 | tf_op jit(solution)/shard_map/all_to_all | solution.py:163
  507.9 3.5 all-to-all-start.8
  512.4 2.3 copy.78
  514.7 21.9 %all-to-all-done.8 = bf16[4,256,2,256]{1,3,2,0:T(8,128)(2,1)S(1)} async-done(((bf16[4,256,2,256]{1,3,2,0:T(8,128)(2,1)}), bf16[4,256,2,256]{1,3,2,0:T(8,128)(2,1)S(1)}, u32[]{:S(2)}, u32[]{:S(2)}) %all-to-all-start.8) | async-done | bytes 1048608 | tf_op jit(solution)/shard_map/all_to_all | solution.py:163
  537.8 1.6 maximum_bitcast_fusion
  539.4 5.8 %copy.84 = bf16[1,1,3,256,2,1024]{5,4,3,2,1,0:T(2,128)(2,1)} copy(bf16[1,1,3,256,2,1024]{3,5,4,2,1,0:T(8,128)(2,1)S(1)} %maximum_bitcast_fusion) | data formatting | bytes 6291456 | tf_op jit(solution)/shard_map/broadcast_in_dim | solution.py:165
  (95 shorter events, 17.6 us)
Async XLA Ops:
  19.1 1.4 copy-start.20
  50.6 30.7 %all-to-all-start = ((s32[64,1,48]{2,1,0:T(1,128)}), s32[64,1,48]{2,1,0:T(1,128)S(1)}, u32[]{:S(2)}, u32[]{:S(2)}) async-start(s32[64,1,48]{2,1,0:T(1,128)} %bitcast.6), calls=%async_computation | async-start | bytes 65536 | tf_op jit(solution)/shard_map/all_to_all | solution.py:102
  81.3 43.6 %all-to-all-start.1 = ((bf16[64,48,256]{2,1,0:T(8,128)(2,1)}), bf16[64,48,256]{2,1,0:T(8,128)(2,1)S(1)}, u32[]{:S(2)}, u32[]{:S(2)}) async-start(bf16[64,48,256]{2,1,0:T(8,128)(2,1)} %bitcast.8), calls=%async_computation.1 | async-start | bytes 3145728 | tf_op jit(solution)/shard_map/all_to_all | solution.py:99
  94.1 6.1 %copy-start.22 = (s32[1,3]{1,0:T(1,128)S(1)}, s32[1,3]{1,0:T(1,128)}, u32[]{:S(2)}) copy-start(s32[1,3]{1,0:T(1,128)} %param.10) | copy-start | bytes 40
  94.1 6.1 %copy-start.23 = (s32[1,3]{1,0:T(1,128)S(1)}, s32[1,3]{1,0:T(1,128)}, u32[]{:S(2)}) copy-start(s32[1,3]{1,0:T(1,128)} %param.9) | copy-start | bytes 40
  138.8 3.0 copy-start.14
  138.8 3.0 copy-start.15
  145.6 52.7 %all-to-all-start.2 = ((bf16[3,512,2,256]{3,2,0,1:T(2,128)(2,1)}), bf16[3,512,2,256]{3,2,0,1:T(2,128)(2,1)}, u32[]{:S(2)}, u32[]{:S(2)}) async-start(bf16[3,512,2,256]{3,2,0,1:T(2,128)(2,1)} %copy.65), calls=%async_computation.2 | async-start | bytes 3145728 | tf_op jit(solution)/shard_map/all_to_all | solution.py:125
  169.4 9.3 %copy-start.5 = (bf16[4,128,2,512]{3,2,1,0:T(2,128)(2,1)S(1)}, bf16[4,128,2,512]{3,2,1,0:T(2,128)(2,1)}, u32[]{:S(2)}) copy-start(bf16[4,128,2,512]{3,2,1,0:T(2,128)(2,1)} %param.12) | copy-start | bytes 3145732
  203.0 4.5 copy-start.6
  203.0 4.5 copy-start.7
  203.0 4.5 copy-start.17
  203.0 4.5 copy-start.21
  207.5 5.6 %copy-start.9 = (f32[128,512]{1,0:T(8,128)}, f32[128,512]{1,0:T(8,128)S(1)}, u32[]{:S(2)}) copy-start(f32[128,512]{1,0:T(8,128)S(1)} %get-tuple-element.32) | copy-start | bytes 786436
  213.2 14.4 %collective-permute-start = (bf16[4,128,2,512]{3,1,2,0:T(8,128)(2,1)S(1)}, bf16[4,128,2,512]{3,1,2,0:T(8,128)(2,1)}, u32[]{:S(2)}, u32[]{:S(2)}) collective-permute-start(bf16[4,128,2,512]{3,1,2,0:T(8,128)(2,1)S(1)} %pad_maximum_fusion.5), channel_id=1, source_target_pairs={{0,252},{4,0},{8,4},{12,8},{16,12},{20,16},{24,20},{28,24},{32,28}... | collective-permute-start | bytes 3145736 | tf_op jit(solution)/shard_map/ppermute | solution.py:19
  227.6 38.8 %collective-permute-start.1 = (bf16[4,128,2,512]{3,1,2,0:T(8,128)(2,1)}, bf16[4,128,2,512]{3,1,2,0:T(8,128)(2,1)}, u32[]{:S(2)}, u32[]{:S(2)}) collective-permute-start(bf16[4,128,2,512]{3,1,2,0:T(8,128)(2,1)} %collective-permute-done), channel_id=1, source_target_pairs={{0,252},{4,0},{8,4},{12,8},{16,12},{20,16},{24,20},{28,24},{32,28}... | collective-permute-start | bytes 3145736 | tf_op jit(solution)/shard_map/ppermute | solution.py:19
  269.7 1.4 copy-start.13
  271.2 1.3 copy-start.18
  272.6 6.7 %copy-start.4 = (bf16[1024,2048]{0,1:T(8,128)(2,1)S(1)}, bf16[1024,2048]{0,1:T(8,128)(2,1)}, u32[]{:S(2)}) copy-start(bf16[1024,2048]{0,1:T(8,128)(2,1)} %fusion.1) | copy-start | bytes 12582916
  272.6 6.7 %copy-start.19 = (bf16[4,128,2,512]{1,3,2,0:T(8,128)(2,1)S(1)}, bf16[4,128,2,512]{1,3,2,0:T(8,128)(2,1)}, u32[]{:S(2)}) copy-start(bf16[4,128,2,512]{1,3,2,0:T(8,128)(2,1)} %copy.74) | copy-start | bytes 3145732
  279.3 4.4 copy-start.12
  284.7 4.8 copy-start.2
  284.7 4.8 copy-start.3
  284.7 4.8 copy-start.10
  284.7 4.9 copy-start.11
  297.3 47.2 %all-to-all-start.3 = ((bf16[4,128,2,1024]{1,2,0,3:T(2,128)(2,1)}), bf16[4,128,2,1024]{1,2,0,3:T(2,128)(2,1)S(1)}, u32[]{:S(2)}, u32[]{:S(2)}) async-start(bf16[4,128,2,1024]{1,2,0,3:T(2,128)(2,1)} %copy.71), calls=%async_computation.3 | async-start | bytes 4194304 | tf_op jit(solution)/shard_map/all_to_all | solution.py:160
  344.5 1.4 copy-start
  345.9 51.3 %all-to-all-start.5 = ((bf16[4,128,2,1024]{1,2,0,3:T(2,128)(2,1)}), bf16[4,128,2,1024]{1,2,0,3:T(2,128)(2,1)S(1)}, u32[]{:S(2)}, u32[]{:S(2)}) async-start(bf16[4,128,2,1024]{1,2,0,3:T(2,128)(2,1)} %copy.76), calls=%async_computation.5 | async-start | bytes 4194304 | tf_op jit(solution)/shard_map/all_to_all | solution.py:160
  397.2 52.2 %all-to-all-start.7 = ((bf16[4,128,2,1024]{1,2,0,3:T(2,128)(2,1)}), bf16[4,128,2,1024]{1,2,0,3:T(2,128)(2,1)}, u32[]{:S(2)}, u32[]{:S(2)}) async-start(bf16[4,128,2,1024]{1,2,0,3:T(2,128)(2,1)} %copy.81), calls=%async_computation.7 | async-start | bytes 4194304 | tf_op jit(solution)/shard_map/all_to_all | solution.py:160
  403.8 2.0 copy-start.1
  405.0 7.8 %copy-start.16 = (f32[256,1,2,512]{3,0,2,1:T(8,128)}, f32[256,1,2,512]{3,0,2,1:T(8,128)S(1)}, u32[]{:S(2)}) copy-start(f32[256,1,2,512]{3,0,2,1:T(8,128)S(1)} %get-tuple-element.29) | copy-start | bytes 3145732
  449.4 29.0 %all-to-all-start.4 = ((bf16[4,256,2,256]{1,3,2,0:T(8,128)(2,1)}), bf16[4,256,2,256]{1,3,2,0:T(8,128)(2,1)S(1)}, u32[]{:S(2)}, u32[]{:S(2)}) async-start(bf16[4,256,2,256]{1,3,2,0:T(8,128)(2,1)} %fusion.34), calls=%async_computation.4 | async-start | bytes 2097152 | tf_op jit(solution)/shard_map/all_to_all | solution.py:163
  478.3 29.5 %all-to-all-start.6 = ((bf16[4,256,2,256]{1,3,2,0:T(8,128)(2,1)}), bf16[4,256,2,256]{1,3,2,0:T(8,128)(2,1)}, u32[]{:S(2)}, u32[]{:S(2)}) async-start(bf16[4,256,2,256]{1,3,2,0:T(8,128)(2,1)} %fusion.37), calls=%async_computation.6 | async-start | bytes 2097152 | tf_op jit(solution)/shard_map/all_to_all | solution.py:163
  507.9 28.7 %all-to-all-start.8 = ((bf16[4,256,2,256]{1,3,2,0:T(8,128)(2,1)}), bf16[4,256,2,256]{1,3,2,0:T(8,128)(2,1)S(1)}, u32[]{:S(2)}, u32[]{:S(2)}) async-start(bf16[4,256,2,256]{1,3,2,0:T(8,128)(2,1)} %fusion.40), calls=%async_computation.8 | async-start | bytes 2097152 | tf_op jit(solution)/shard_map/all_to_all | solution.py:163
  536.6 1.2 copy-start.8
where the time goes:
time: 555 us; the launch traced here: 546 us
  waiting for transfers between devices  203 us (37%)
  other arithmetic  120 us (22%)
  local copies, waits for them, and re-layouts  108 us (19%)
  starting transfers between devices  78.6 us (14%)
  matrix products  35.7 us (6%)
    all_to_all x3, waiting for transfers between devices, body(): lax.all_to_all(turned_back, 'det', split_axis=3, concat_axis=1, tiled=True)  106 us
    all_to_all x3, waiting for transfers between devices, body(): lax.all_to_all(partial_value, 'det', split_axis=0, concat_axis=3, tiled=T...  52.9 us
    another operation x7, other arithmetic  31.7 us
    sin x3, other arithmetic, phases(): return (jnp.cos(phase_angle), jnp.sin(phase_angle))  23 us
    all_to_all x1, waiting for transfers between devices, body(): lax.all_to_all(send_rows.astype(jnp.bfloat16), 'seg', split_axis=0, conca...  20.1 us
    all_to_all x6, local copies, waits for them, and re-layouts, body(): lax.all_to_all(turned_back, 'det', split_axis=3, concat_axis=1, tiled=True)  18.2 us
    gather x1, local copies, waits for them, and re-layouts, body(): chosen = padded_target[source]  17.4 us
    neg x2, other arithmetic, rotation_table(): lower_rows = jnp.concatenate([-sine_value, cosine], axis=1)  17.1 us
  transfers between devices with their start and end apart: 11, of which 9 were waited for; matrix products, arithmetic and copies ran while one was open for 25% of the time, Pallas kernels for 0%

commit v1 on v0

v1 whole, which is shorter than its diff:
```python
import functools
import math

import jax
import jax.numpy as jnp
import numpy as np
from jax import lax
from jax.experimental import pallas as pl
from jax.experimental.pallas import tpu as pltpu
from jax.sharding import PartitionSpec as P

V = 512
U = 1024
DETECTORS = 3
BLOCK = 4
STEPS = 3
SAMPLES = 524288
SEGS = 64
DETS = 4
SLOTS = 3072
CAP = 48
QU = U // DETS
QV = V // DETS
ROWS = DETECTORS * V
HALF = U // 2
MESH = pl.DeviceIdType.MESH
F32 = jnp.float32
BF16 = jnp.bfloat16
LIMIT = 60 * 1024 * 1024
VM = pl.BlockSpec(memory_space=pltpu.VMEM)
SM = pl.BlockSpec(memory_space=pltpu.SMEM)
HB = pl.BlockSpec(memory_space=pl.ANY)


def angles(rows, cols, modulus, direction):
    residue = (rows[:, None].astype(np.int64) * cols[None, :]) % modulus
    angle = np.float32(direction * 2.0 * math.pi / modulus) * residue.astype(np.float32)
    return np.cos(angle), np.sin(angle)


@functools.cache
def tables():
    v, u, m = np.arange(V), np.arange(U), np.arange(HALF)
    bf = np.dtype(jnp.bfloat16)
    c, s = angles(v, v, V, -1.0)
    row = (np.concatenate([c, s], 0) / math.sqrt(V)).astype(bf)
    twist = np.stack([*angles(v, u, SAMPLES, -1.0)])
    twist = twist.reshape(2, V, DETS, QU).transpose(2, 0, 1, 3).astype(np.float32)
    c, s = angles(u, m, U, -1.0)
    col = np.stack([np.concatenate([c, s], 1), np.concatenate([-s, c], 1)])
    col = (col / math.sqrt(U)).reshape(2, DETS, QU, U).transpose(1, 0, 2, 3)
    col = col.reshape(DETS, 2 * QU, U).astype(bf)
    c, s = angles(m, u, U, 1.0)
    back = np.concatenate([np.concatenate([c, s], 1), np.concatenate([-s, c], 1)], 0)
    back = (back / math.sqrt(U)).astype(bf)
    untwist = np.stack([*angles(v, u, SAMPLES, 1.0)]).astype(np.float32)
    c, s = angles(np.arange(V // 4, 3 * V // 4), v, V, 1.0)
    last = np.stack([np.concatenate([c, -s], 1), np.concatenate([s, c], 1)], 1)
    last = (last / math.sqrt(V)).reshape(V, 2 * V).astype(bf)
    return row, twist, col, back, untwist, last


def sort_kernel(me_ref, target_ref, strain_ref, rows_ref, ids_ref, held, dest):
    held[...] = strain_ref[...].astype(BF16)
    block = 256
    count = SLOTS // block
    lane = lax.broadcasted_iota(jnp.int32, (block, block), 1)
    sub = lax.broadcasted_iota(jnp.int32, (block, block), 0)
    upper = jnp.where(sub <= lane, 1.0, 0.0).astype(BF16)
    seg = lax.broadcasted_iota(jnp.int32, (SEGS, block), 0)
    carry = jnp.zeros((SEGS, 1), F32)
    high = jnp.zeros((SEGS, SEGS), F32)
    low = jnp.zeros((SEGS, SEGS), F32)
    for b in range(count):
        t = target_ref[b : b + 1, :]
        owner = ((t >> 9) * 43691) >> 17
        owner = jnp.where(t >= 0, owner, SEGS)
        local = t - owner * ROWS
        mine = jnp.where(seg == owner, 1.0, 0.0)
        before = jnp.dot(mine.astype(BF16), upper, preferred_element_type=F32)
        rank = jnp.sum(mine * (before + carry), axis=0, keepdims=True).astype(jnp.int32) - 1
        carry = carry + jnp.sum(mine, axis=1, keepdims=True)
        dest[b : b + 1, :] = jnp.where(t >= 0, owner * CAP + rank, -1)
        order = jnp.where(seg == rank, 1.0, 0.0).astype(BF16)
        spread = (((1,), (1,)), ((), ()))
        upper_part = (mine * ((local >> 6) + 1).astype(F32)).astype(BF16)
        lower_part = (mine * (local & 63).astype(F32)).astype(BF16)
        high = high + lax.dot_general(upper_part, order, spread, preferred_element_type=F32)
        low = low + lax.dot_general(lower_part, order, spread, preferred_element_type=F32)
    ids = jnp.where(high > 0.5, high * 64.0 + low - 63.0, 0.0).astype(jnp.int32)
    ids = jnp.concatenate([ids, ids], axis=1)
    side = lax.broadcasted_iota(jnp.int32, (SEGS, 128), 1) // 64
    parity = (lax.broadcasted_iota(jnp.int32, (SEGS, 128), 0) + me_ref[0]) & 1
    ids_ref[...] = jnp.where(side == parity, ids, 0)
    step = 512

    def place(i, _):
        want = lax.broadcasted_iota(jnp.int32, (step, block), 0) + i * step
        chosen = [
            jnp.where(want == dest[b : b + 1, :], 1.0, 0.0).astype(BF16) for b in range(count)
        ]
        rows = jnp.dot(jnp.concatenate(chosen, axis=1), held[...], preferred_element_type=F32)
        rows_ref[pl.ds(i * step, step), :] = rows.astype(BF16)
        return 0

    lax.fori_loop(0, SLOTS // step, place, 0)


def sort_rows(me, target, strain):
    return pl.pallas_call(
        sort_kernel,
        out_shape=(
            jax.ShapeDtypeStruct((SLOTS, QU), BF16),
            jax.ShapeDtypeStruct((SEGS, 128), jnp.int32),
        ),
        in_specs=[SM, VM, VM],
        out_specs=(VM, VM),
        scratch_shapes=[
            pltpu.VMEM((SLOTS, QU), BF16),
            pltpu.VMEM((SLOTS // 256, 256), jnp.int32),
        ],
        compiler_params=pltpu.CompilerParams(vmem_limit_bytes=LIMIT),
        cost_estimate=pl.CostEstimate(
            flops=2 * SLOTS * SLOTS * QU, bytes_accessed=SLOTS * QU * 6, transcendentals=0
        ),
        name="sort_rows",
    )(me, target, strain)


GROUP = 16


def route_kernel(
    rows_ref, ids_ref, bank_ref, placed_ref, full_ref,
    arrived, arrived_ids, chosen, total,
    row_send, row_recv, id_send, id_recv, bank_send, bank_recv, own_sem,
):
    me = lax.axis_index("seg")
    det = lax.axis_index("det")
    barrier = pltpu.get_barrier_semaphore()

    def greet(o, _):
        pl.semaphore_signal(
            barrier, inc=1, device_id={"seg": (me + o) % SEGS}, device_id_type=MESH
        )
        return 0

    lax.fori_loop(1, SEGS, greet, 0)
    for o in range(1, DETS):
        pl.semaphore_signal(
            barrier, inc=1, device_id={"det": (det + o) % DETS}, device_id_type=MESH
        )
    own_rows = pltpu.make_async_copy(rows_ref.at[me], arrived.at[0, pl.ds(0, CAP)], own_sem.at[0])
    own_rows.start()
    own_ids = pltpu.make_async_copy(ids_ref.at[me], arrived_ids.at[0], own_sem.at[1])
    own_ids.start()
    own_bank = pltpu.make_async_copy(
        bank_ref.at[det], full_ref.at[pl.ds(det * QV, QV)], own_sem.at[2]
    )
    own_bank.start()
    arrived[:, CAP:, :] = jnp.zeros((SEGS, 64 - CAP, QU), BF16)
    pl.semaphore_wait(barrier, SEGS + DETS - 2)

    def bank_copy(o):
        other = (det + o) % DETS
        return pltpu.make_async_remote_copy(
            src_ref=bank_ref.at[other],
            dst_ref=full_ref.at[pl.ds(det * QV, QV)],
            send_sem=bank_send.at[o],
            recv_sem=bank_recv.at[o],
            device_id={"det": other},
            device_id_type=MESH,
        )

    def row_copy(o):
        other = (me + o) % SEGS
        return pltpu.make_async_remote_copy(
            src_ref=rows_ref.at[other],
            dst_ref=arrived.at[o, pl.ds(0, CAP)],
            send_sem=row_send.at[o],
            recv_sem=row_recv.at[o],
            device_id={"seg": other},
            device_id_type=MESH,
        )

    def id_copy(o):
        other = (me + o) % SEGS
        return pltpu.make_async_remote_copy(
            src_ref=ids_ref.at[other],
            dst_ref=arrived_ids.at[o],
            send_sem=id_send.at[o],
            recv_sem=id_recv.at[o],
            device_id={"seg": other},
            device_id_type=MESH,
        )

    def send(o, _):
        id_copy(o).start()
        row_copy(o).start()
        return 0

    lax.fori_loop(1, SEGS, send, 0)
    for o in range(1, DETS):
        bank_copy(o).start()
    own_rows.wait()
    own_ids.wait()

    def receive(o, _):
        id_copy(o).wait_recv()
        row_copy(o).wait_recv()
        return 0

    wide = GROUP * 64

    for g in range(SEGS // GROUP):
        lax.fori_loop(max(1, g * GROUP), (g + 1) * GROUP, receive, 0)
        idents = [
            arrived_ids[g * GROUP + 2 * p] + arrived_ids[g * GROUP + 2 * p + 1] - 1
            for p in range(GROUP // 2)
        ]
        for p in range(GROUP // 2):
            chosen[:, p * 128 : (p + 1) * 128] = jnp.where(
                lax.broadcasted_iota(jnp.int32, (ROWS, 128), 0) == idents[p], 1.0, 0.0
            ).astype(BF16)
        block = arrived[g * GROUP : (g + 1) * GROUP].reshape(wide, QU)
        part = jnp.dot(chosen[...], block, preferred_element_type=F32)
        if g == 0:
            total[...] = part
        elif g < SEGS // GROUP - 1:
            total[...] += part
        else:
            placed_ref[...] = (total[...] + part).astype(BF16)

    own_bank.wait()
    for o in range(1, DETS):
        bank_copy(o).wait()

    def sent(o, _):
        id_copy(o).wait_send()
        row_copy(o).wait_send()
        return 0

    lax.fori_loop(1, SEGS, sent, 0)


def route_rows(rows, ids, bank):
    return pl.pallas_call(
        route_kernel,
        out_shape=(
            jax.ShapeDtypeStruct((ROWS, QU), BF16),
            jax.ShapeDtypeStruct((V, U), BF16),
        ),
        in_specs=[VM, VM, HB],
        out_specs=(VM, HB),
        scratch_shapes=[
            pltpu.VMEM((SEGS, 64, QU), BF16),
            pltpu.VMEM((SEGS, 1, 128), jnp.int32),
            pltpu.VMEM((ROWS, GROUP * 64), BF16),
            pltpu.VMEM((ROWS, QU), F32),
            pltpu.SemaphoreType.DMA((SEGS,)),
            pltpu.SemaphoreType.DMA((SEGS,)),
            pltpu.SemaphoreType.DMA((SEGS,)),
            pltpu.SemaphoreType.DMA((SEGS,)),
            pltpu.SemaphoreType.DMA((DETS,)),
            pltpu.SemaphoreType.DMA((DETS,)),
            pltpu.SemaphoreType.DMA((3,)),
        ],
        compiler_params=pltpu.CompilerParams(
            vmem_limit_bytes=LIMIT, collective_id=0, has_side_effects=True
        ),
        cost_estimate=pl.CostEstimate(
            flops=2 * ROWS * 4096 * QU, bytes_accessed=SLOTS * QU * 4, transcendentals=0
        ),
        name="route_rows",
    )(rows, ids, bank)


def section_kernel(
    gate_ref, shift_ref, placed_ref, full_ref, row_ref, twist_ref, turned_ref, shifted_ref,
    twist, sem,
):
    det = lax.axis_index("det")
    fetch = pltpu.make_async_copy(twist_ref.at[det], twist, sem)
    fetch.start()
    shift = shift_ref[det]
    k = lax.broadcasted_iota(jnp.int32, (V, 128), 0)
    angle = (-2.0 * math.pi / SAMPLES) * ((k * shift) % SAMPLES).astype(F32)
    row_cos, row_sin = jnp.cos(angle)[:, :1], jnp.sin(angle)[:, :1]
    m = lax.broadcasted_iota(jnp.int32, (8, HALF), 1)
    angle = (-2.0 * math.pi / U) * ((m * shift) % U).astype(F32)
    col_cos, col_sin = jnp.cos(angle)[:1], jnp.sin(angle)[:1]
    real = full_ref[:, :HALF].astype(F32)
    imag = full_ref[:, HALF:].astype(F32)
    cosine = row_cos * col_cos - row_sin * col_sin
    sine = row_cos * col_sin + row_sin * col_cos
    shifted_ref[:, :HALF] = (real * cosine - imag * sine).astype(BF16)
    shifted_ref[:, HALF:] = (real * sine + imag * cosine).astype(BF16)
    sample = lax.broadcasted_iota(jnp.int32, (V, QU), 0) * U
    sample = sample + lax.broadcasted_iota(jnp.int32, (V, QU), 1) + det * QU
    fetch.wait()
    for d in range(DETECTORS):
        begin = gate_ref[0, d]
        end = begin + gate_ref[1, d]
        inside = (sample >= begin) & (sample < end)
        gated = jnp.where(inside, 0.0, placed_ref[d * V : (d + 1) * V].astype(F32)).astype(BF16)
        folded = jnp.dot(row_ref[...], gated, preferred_element_type=F32)
        real, imag = folded[:V], folded[V:]
        cosine, sine = twist[0], twist[1]
        first = (real * cosine - imag * sine).astype(BF16)
        second = (real * sine + imag * cosine).astype(BF16)
        for q in range(DETS):
            turned_ref[q, d * QV : (d + 1) * QV, :QU] = first[q * QV : (q + 1) * QV]
            turned_ref[q, d * QV : (d + 1) * QV, QU:] = second[q * QV : (q + 1) * QV]


def first_section(gates, shift, placed, full, row, twist):
    return pl.pallas_call(
        section_kernel,
        out_shape=(
            jax.ShapeDtypeStruct((DETS, DETECTORS * QV, 2 * QU), BF16),
            jax.ShapeDtypeStruct((V, U), BF16),
        ),
        in_specs=[SM, SM, VM, VM, VM, HB],
        out_specs=(VM, VM),
        scratch_shapes=[pltpu.VMEM((2, V, QU), F32), pltpu.SemaphoreType.DMA],
        compiler_params=pltpu.CompilerParams(vmem_limit_bytes=LIMIT),
        name="first_section",
    )(gates, shift, placed, full, row, twist)


def spectrum_kernel(
    turned_ref, shifted_ref, psd_ref, col_ref, coherent_ref, next_ref, after_ref,
    arrived, mine, total, turn_send, turn_recv, coh_send, coh_recv, pass_send, pass_recv, own_sem,
):
    me = lax.axis_index("seg")
    det = lax.axis_index("det")
    barrier = pltpu.get_barrier_semaphore()
    for o in (1, 2, SEGS - 2, SEGS - 1):
        pl.semaphore_signal(
            barrier, inc=1, device_id={"seg": (me + o) % SEGS}, device_id_type=MESH
        )
    for o in range(1, DETS):
        pl.semaphore_signal(
            barrier, inc=1, device_id={"det": (det + o) % DETS}, device_id_type=MESH
        )
    own = pltpu.make_async_copy(turned_ref.at[det], arrived.at[0], own_sem.at[0])
    own.start()
    pl.semaphore_wait(barrier, 4 + DETS - 1)

    def turn_copy(o):
        other = (det + o) % DETS
        return pltpu.make_async_remote_copy(
            src_ref=turned_ref.at[other],
            dst_ref=arrived.at[o],
            send_sem=turn_send.at[o],
            recv_sem=turn_recv.at[o],
            device_id={"det": other},
            device_id_type=MESH,
        )

    def pass_copy(o, dst_ref):
        return pltpu.make_async_remote_copy(
            src_ref=shifted_ref,
            dst_ref=dst_ref,
            send_sem=pass_send.at[o],
            recv_sem=pass_recv.at[o],
            device_id={"seg": (me + SEGS - o) % SEGS},
            device_id_type=MESH,
        )

    def coherent_copy(o):
        return pltpu.make_async_remote_copy(
            src_ref=mine,
            dst_ref=coherent_ref.at[pl.ds(det * QV, QV)],
            send_sem=coh_send.at[o],
            recv_sem=coh_recv.at[o],
            device_id={"det": (det + o) % DETS},
            device_id_type=MESH,
        )

    for o in (2, 1, 3):
        turn_copy(o).start()
    pass_copy(1, next_ref).start()
    pass_copy(2, after_ref).start()
    own.wait()
    total[...] = jnp.dot(arrived[0], col_ref[det], preferred_element_type=F32)
    for o in (1, 3, 2):
        turn_copy(o).wait_recv()
        part = jnp.dot(
            arrived[o], col_ref[(det + DETS - o) % DETS], preferred_element_type=F32
        )
        total[...] += part
    for half in range(2):
        cols = slice(half * HALF, (half + 1) * HALF)
        value = psd_ref[0] * total[:QV, cols]
        for d in range(1, DETECTORS):
            value = value + psd_ref[d] * total[d * QV : (d + 1) * QV, cols]
        mine[:, cols] = value.astype(BF16)
    for o in (2, 1, 3):
        coherent_copy(o).start()
    keep = pltpu.make_async_copy(mine, coherent_ref.at[pl.ds(det * QV, QV)], own_sem.at[1])
    keep.start()
    for o in (1, 2, 3):
        turn_copy(o).wait_send()
        coherent_copy(o).wait()
    keep.wait()
    pass_copy(1, next_ref).wait()
    pass_copy(2, after_ref).wait()


def spectra(turned, shifted, psd, col):
    bank = jax.ShapeDtypeStruct((V, U), BF16)
    return pl.pallas_call(
        spectrum_kernel,
        out_shape=(bank, bank, bank),
        in_specs=[VM, HB, VM, VM],
        out_specs=(HB, HB, HB),
        scratch_shapes=[
            pltpu.VMEM((DETS, DETECTORS * QV, 2 * QU), BF16),
            pltpu.VMEM((QV, U), BF16),
            pltpu.VMEM((DETECTORS * QV, U), F32),
            pltpu.SemaphoreType.DMA((DETS,)),
            pltpu.SemaphoreType.DMA((DETS,)),
            pltpu.SemaphoreType.DMA((DETS,)),
            pltpu.SemaphoreType.DMA((DETS,)),
            pltpu.SemaphoreType.DMA((STEPS,)),
            pltpu.SemaphoreType.DMA((STEPS,)),
            pltpu.SemaphoreType.DMA((2,)),
        ],
        compiler_params=pltpu.CompilerParams(
            vmem_limit_bytes=LIMIT, collective_id=1, has_side_effects=True
        ),
        cost_estimate=pl.CostEstimate(
            flops=2 * DETECTORS * QV * 2 * U * U, bytes_accessed=8 * V * U, transcendentals=0
        ),
        name="spectra",
    )(turned, shifted, psd, col)


def inverse_kernel(coherent_ref, shifted_ref, back_ref, untwist_ref, last_ref, out_ref, partial):
    real, imag = coherent_ref[:, :HALF].astype(F32), coherent_ref[:, HALF:].astype(F32)
    other_real = shifted_ref[:, :HALF].astype(F32)
    other_imag = shifted_ref[:, HALF:].astype(F32)
    product = jnp.concatenate(
        [
            (real * other_real + imag * other_imag).astype(BF16),
            (imag * other_real - real * other_imag).astype(BF16),
        ],
        axis=1,
    )
    series = jnp.dot(product, back_ref[...], preferred_element_type=F32)
    cosine, sine = untwist_ref[0], untwist_ref[1]
    partial[:V] = (series[:, :U] * cosine - series[:, U:] * sine).astype(BF16)
    partial[V:] = (series[:, :U] * sine + series[:, U:] * cosine).astype(BF16)
    out_ref[...] = jnp.dot(last_ref[...], partial[...], preferred_element_type=F32).astype(BF16)


def inverse_step(coherent, shifted, back, untwist, last):
    return pl.pallas_call(
        inverse_kernel,
        out_shape=jax.ShapeDtypeStruct((V, U), BF16),
        in_specs=[VM] * 5,
        out_specs=VM,
        scratch_shapes=[pltpu.VMEM((2 * V, U), BF16)],
        compiler_params=pltpu.CompilerParams(vmem_limit_bytes=LIMIT),
        name="inverse_step",
    )(coherent, shifted, back, untwist, last)


def body(strain, row_target, gate_start, gate_width, inverse_psd, templates, template_shift):
    row, twist, col, back, untwist, last = (jnp.asarray(t) for t in tables())
    me = lax.axis_index("seg").astype(jnp.int32).reshape(1)
    rows, ids = sort_rows(me, row_target.reshape(SLOTS // 256, 256), strain)
    placed, full = route_rows(
        rows.reshape(SEGS, CAP, QU),
        ids.reshape(SEGS, 1, 128),
        templates.reshape(BLOCK, QV, U),
    )
    gates = jnp.concatenate([gate_start, gate_width], axis=0)
    turned, shifted = first_section(gates, template_shift, placed, full, row, twist)
    coherent, following, after = spectra(turned, shifted, inverse_psd, col)
    results = [
        inverse_step(coherent, bank, back, untwist, last) for bank in (shifted, following, after)
    ]
    return jnp.stack(results, axis=0).reshape(1, 1, STEPS, V // 2, 2, U)


def solution(mesh):
    in_specs = (
        P("seg", "det"),
        P("seg"),
        P("seg", None),
        P("seg", None),
        P(None, "det", None),
        P("seg", "det", None, None),
        P("seg"),
    )
    out_specs = P("seg", "det", None, None, None, None)
    return jax.shard_map(body, mesh=mesh, in_specs=in_specs, out_specs=out_specs, check_vma=False)
```

time: 555 us -> 276 us (0.50); the launches traced: 546 us -> 275 us
  Pallas kernels: 0 us -> 258 us
  waiting for transfers between devices: 203 us -> 0 us
  other arithmetic: 120 us -> 8.8 us
  local copies, waits for them, and re-layouts: 108 us -> 8.26 us
  starting transfers between devices: 78.6 us -> 0 us
  matrix products: 35.7 us -> 0 us
    pallas_call x0 -> x7, Pallas kernels: none -> 258 us  [the longest x1 137 us: spectra(): pl.pallas_call(spectrum_kernel, out_shape=(bank, bank, bank), in_specs=[V...]
    all_to_all x9 -> x0, waiting for transfers between devices: 189 us -> none  [the longest x3 106 us: body(): lax.all_to_all(turned_back, 'det', split_axis=3, concat_axis=1, tiled=True)]
    all_to_all x9 -> x0, starting transfers between devices: 66.3 us -> none  [the longest x1 15.6 us: body(): lax.all_to_all(send_index, 'seg', split_axis=0, concat_axis=0, tiled=True)]
    dot_general x8 -> x0, matrix products: 35.7 us -> none  [the longest x3 15.9 us: body(): jnp.dot(product.reshape(BLOCK * depth_local, U), inverse_columns, preferr...]
    another operation x16 -> x1, other arithmetic: 39.5 us -> 7.6 us  [body(): return jnp.stack(results, axis=0).reshape(1, 1, STEPS, V // 2, 2, U)]
    gather x2 -> x0, local copies, waits for them, and re-layouts: 30.5 us -> none  [the longest x1 17.4 us: body(): chosen = padded_target[source]]
    all_to_all x11 -> x0, local copies, waits for them, and re-layouts: 25.5 us -> none  [the longest x6 18.2 us: body(): lax.all_to_all(turned_back, 'det', split_axis=3, concat_axis=1, tiled=True)]
    sin x3 -> x0, other arithmetic: 23 us -> none  [phases(): return (jnp.cos(phase_angle), jnp.sin(phase_angle))]
  transfers between devices with their start and end apart: 11 -> 0, of which waited for: 9 -> 0; matrix products, arithmetic and copies ran while one was open for 25% -> 0% of each run, Pallas kernels for 0% -> 0%
where the time goes in v1:
time: 276 us; the launch traced here: 275 us
  Pallas kernels  258 us (93%)
  other arithmetic  8.8 us (3%)
  local copies, waits for them, and re-layouts  8.26 us (3%)
    pallas_call x1, Pallas kernels, spectra(): pl.pallas_call(spectrum_kernel, out_shape=(bank, bank, bank), in_specs=[V...  137 us
    pallas_call x1, Pallas kernels, route_rows(): pl.pallas_call(route_kernel, out_shape=(jax.ShapeDtypeStruct((ROWS, QU),...  76 us
    pallas_call x3, Pallas kernels, inverse_step(): pl.pallas_call(inverse_kernel, out_shape=jax.ShapeDtypeStruct((V, U), BF1...  27.5 us
    pallas_call x1, Pallas kernels, sort_rows(): pl.pallas_call(sort_kernel, out_shape=(jax.ShapeDtypeStruct((SLOTS, QU),...  11.5 us
    another operation x1, other arithmetic, body(): return jnp.stack(results, axis=0).reshape(1, 1, STEPS, V // 2, 2, U)  7.6 us
    pallas_call x1, Pallas kernels, first_section(): pl.pallas_call(section_kernel, out_shape=(jax.ShapeDtypeStruct((DETS, DET...  5.92 us

profile of v1, /device:TPU:1, one launch (start us, length us, event | category | flops | bytes accessed | tf_op | source)
XLA Modules:
  0.0 275.4 jit_solution(145221885520723955)
XLA Ops:
  0.0 1.2 pad_add_fusion.gate_ref
  1.2 1.3 reshape.23.target_ref
  2.5 2.6 reshape.26.bank_ref
  5.1 11.5 %sort_rows.1 = (bf16[3072,256]{1,0:T(8,128)(2,1)}, s32[64,128]{1,0:T(8,128)}) custom-call(s32[1]{0:T(128)} %bitcast.me_ref, s32[12,256]{1,0:T(8,128)} %reshape.23.target_ref, f32[3072,256]{1,0:T(8,128)} %strain_ref.1), custom_call_target="tpu_custom_call" | custom-call | flops 4831838208 | bytes 4718592 | tf_op jit(solution)/shard_map/sort_rows/pallas_call | solution.py:110
  16.6 76.0 %route_rows.1 = (bf16[1536,256]{1,0:T(8,128)(2,1)}, bf16[512,1024]{1,0:T(8,128)(2,1)}) custom-call(bf16[64,48,256]{2,1,0:T(8,128)(2,1)} %bitcast.3, s32[64,1,128]{2,1,0:T(1,128)} %bitcast.4, bf16[4,128,1024]{2,1,0:T(8,128)(2,1)} %reshape.26.bank_ref), custom_call_target="tpu_custom_call" | custom-call | flops 3221225472 | bytes 3145728 | tf_op jit(solution)/shard_map/route_rows/pallas_call | solution.py:247
  92.6 5.9 %first_section.1 = (bf16[4,384,512]{2,1,0:T(8,128)(2,1)}, bf16[512,1024]{1,0:T(8,128)(2,1)}) custom-call(s32[2,3]{1,0:T(2,128)} %pad_add_fusion.gate_ref, s32[4]{0:T(128)} %shift_ref.1, bf16[1536,256]{1,0:T(8,128)(2,1)} %get-tuple-element.16.placed_ref, bf16[512,1024]{1,0:T(8,128)(2,1)} %get-tuple-element.17.full_ref, ...), custom_call_target="tpu_custom_call" | custom-call | tf_op jit(solution)/shard_map/first_section/pallas_call | solution.py:317
  98.5 137.4 %spectra.1 = (bf16[512,1024]{1,0:T(8,128)(2,1)}, bf16[512,1024]{1,0:T(8,128)(2,1)}, bf16[512,1024]{1,0:T(8,128)(2,1)}) custom-call(bf16[4,384,512]{2,1,0:T(8,128)(2,1)} %get-tuple-element.18.turned_ref, bf16[512,1024]{1,0:T(8,128)(2,1)} %get-tuple-element.19.shifted_ref, f32[3,128,512]{2,1,0:T(8,128)} %psd_ref.1, bf16[4,512,1024]{2,1,0:T(8,128)(2,1)} %constant.20.clone.col_ref), custom_call_target="tpu_custom_call" | custom-call | flops 1610612736 | bytes 4194304 | tf_op jit(solution)/shard_map/spectra/pallas_call | solution.py:413
  236.0 9.1 %inverse_step.3 = bf16[512,1024]{1,0:T(8,128)(2,1)} custom-call(bf16[512,1024]{1,0:T(8,128)(2,1)} %get-tuple-element.20.coherent_ref, bf16[512,1024]{1,0:T(8,128)(2,1)} %get-tuple-element.19.shifted_ref, bf16[1024,2048]{1,0:T(8,128)(2,1)} %constant.21.clone.back_ref, f32[2,512,1024]{2,1,0:T(8,128)} %constant.22.clone.untwist_ref, ...), custom_call_target="tpu_custom_call" | custom-call | tf_op jit(solution)/shard_map/inverse_step/pallas_call | solution.py:459
  245.1 1.7 stack.12
  246.8 9.1 %inverse_step.4 = bf16[512,1024]{1,0:T(8,128)(2,1)} custom-call(bf16[512,1024]{1,0:T(8,128)(2,1)} %get-tuple-element.20.coherent_ref, bf16[512,1024]{1,0:T(8,128)(2,1)} %get-tuple-element.21.shifted_ref, bf16[1024,2048]{1,0:T(8,128)(2,1)} %constant.21.clone.back_ref, f32[2,512,1024]{2,1,0:T(8,128)} %constant.22.clone.untwist_ref, ...), custom_call_target="tpu_custom_call" | custom-call | tf_op jit(solution)/shard_map/inverse_step/pallas_call | solution.py:459
  255.9 0.0 copy-start
  255.9 9.2 %inverse_step.5 = bf16[512,1024]{1,0:T(8,128)(2,1)} custom-call(bf16[512,1024]{1,0:T(8,128)(2,1)} %get-tuple-element.20.coherent_ref, bf16[512,1024]{1,0:T(8,128)(2,1)} %get-tuple-element.22.shifted_ref, bf16[1024,2048]{1,0:T(8,128)(2,1)} %constant.21.clone.back_ref, f32[2,512,1024]{2,1,0:T(8,128)} %constant.22.clone.untwist_ref, ...), custom_call_target="tpu_custom_call" | custom-call | tf_op jit(solution)/shard_map/inverse_step/pallas_call | solution.py:459
  265.1 1.5 stack.14
  266.6 0.0 copy-done
  266.6 1.2 stack.13
  267.8 7.6 %pad_maximum_fusion = bf16[1,1,3,256,2,1024]{5,4,3,2,1,0:T(2,128)(2,1)} fusion(bf16[1,1,1,256,2,1024]{5,4,3,2,1,0:T(2,128)(2,1)S(1)} %stack.14, bf16[1,1,1,256,2,1024]{5,4,3,2,1,0:T(2,128)(2,1)} %stack.13, bf16[1,1,1,256,2,1024]{5,4,3,2,1,0:T(2,128)(2,1)S(1)} %stack.12), kind=kLoop, calls=%fused_computation | loop fusion | flops 3145728 | bytes 6291456 | tf_op jit(solution)/shard_map/stack | solution.py:485
Async XLA Ops:
  255.9 10.7 %copy-start = (bf16[512,1024]{1,0:T(8,128)(2,1)S(1)}, bf16[512,1024]{1,0:T(8,128)(2,1)}, u32[]{:S(2)}) copy-start(bf16[512,1024]{1,0:T(8,128)(2,1)} %inverse_step.4) | copy-start | bytes 3145732

commit v2 on v1

v2 whole, which is shorter than its diff:
```python
import functools
import math

import jax
import jax.numpy as jnp
import numpy as np
from jax import lax
from jax.experimental import pallas as pl
from jax.experimental.pallas import tpu as pltpu
from jax.sharding import PartitionSpec as P

V = 512
U = 1024
DETECTORS = 3
BLOCK = 4
STEPS = 3
SAMPLES = 524288
SEGS = 64
DETS = 4
SLOTS = 3072
CAP = 48
QU = U // DETS
QV = V // DETS
ROWS = DETECTORS * V
HALF = U // 2
MESH = pl.DeviceIdType.MESH
F32 = jnp.float32
BF16 = jnp.bfloat16
LIMIT = 60 * 1024 * 1024
VM = pl.BlockSpec(memory_space=pltpu.VMEM)
SM = pl.BlockSpec(memory_space=pltpu.SMEM)
HB = pl.BlockSpec(memory_space=pl.ANY)


def angles(rows, cols, modulus, direction):
    residue = (rows[:, None].astype(np.int64) * cols[None, :]) % modulus
    angle = np.float32(direction * 2.0 * math.pi / modulus) * residue.astype(np.float32)
    return np.cos(angle), np.sin(angle)


@functools.cache
def tables():
    v, u, m = np.arange(V), np.arange(U), np.arange(HALF)
    bf = np.dtype(jnp.bfloat16)
    c, s = angles(v, v, V, -1.0)
    row = (np.concatenate([c, s], 0) / math.sqrt(V)).astype(bf)
    twist = np.stack([*angles(v, u, SAMPLES, -1.0)])
    twist = twist.reshape(2, V, DETS, QU).transpose(2, 0, 1, 3).astype(np.float32)
    c, s = angles(u, m, U, -1.0)
    col = np.stack([np.concatenate([c, s], 1), np.concatenate([-s, c], 1)])
    col = (col / math.sqrt(U)).reshape(2, DETS, QU, U).transpose(1, 0, 2, 3)
    col = col.reshape(DETS, 2 * QU, U).astype(bf)
    c, s = angles(m, u, U, 1.0)
    back = np.concatenate([np.concatenate([c, s], 1), np.concatenate([-s, c], 1)], 0)
    back = (back / math.sqrt(U)).astype(bf)
    untwist = np.stack([*angles(v, u, SAMPLES, 1.0)]).astype(np.float32)
    c, s = angles(np.arange(V // 4, 3 * V // 4), v, V, 1.0)
    last = np.stack([np.concatenate([c, -s], 1), np.concatenate([s, c], 1)], 1)
    last = (last / math.sqrt(V)).reshape(V, 2 * V).astype(bf)
    return row, twist, col, back, untwist, last


GROUP = 16
LANES = 256
COUNT = SLOTS // LANES


def sort_ranks(me, target_ref, dest, ids):
    lane = lax.broadcasted_iota(jnp.int32, (LANES, LANES), 1)
    sub = lax.broadcasted_iota(jnp.int32, (LANES, LANES), 0)
    upper = jnp.where(sub <= lane, 1.0, 0.0).astype(BF16)
    seg = lax.broadcasted_iota(jnp.int32, (SEGS, LANES), 0)
    carry = jnp.zeros((SEGS, 1), F32)
    high = jnp.zeros((SEGS, SEGS), F32)
    low = jnp.zeros((SEGS, SEGS), F32)
    spread = (((1,), (1,)), ((), ()))
    for b in range(COUNT):
        t = target_ref[b : b + 1, :]
        owner = ((t >> 9) * 43691) >> 17
        local = t - owner * ROWS
        owner = jnp.where(t >= 0, (owner + SEGS - me) & (SEGS - 1), SEGS)
        mine = jnp.where(seg == owner, 1.0, 0.0)
        before = jnp.dot(mine.astype(BF16), upper, preferred_element_type=F32)
        rank = jnp.sum(mine * (before + carry), axis=0, keepdims=True).astype(jnp.int32) - 1
        carry = carry + jnp.sum(mine, axis=1, keepdims=True)
        dest[b : b + 1, :] = jnp.where(t >= 0, owner * CAP + rank, -1)
        order = jnp.where(seg == rank, 1.0, 0.0).astype(BF16)
        upper_part = (mine * ((local >> 6) + 1).astype(F32)).astype(BF16)
        lower_part = (mine * (local & 63).astype(F32)).astype(BF16)
        high = high + lax.dot_general(upper_part, order, spread, preferred_element_type=F32)
        low = low + lax.dot_general(lower_part, order, spread, preferred_element_type=F32)
    found = jnp.where(high > 0.5, high * 64.0 + low - 63.0, 0.0).astype(jnp.int32)
    found = jnp.concatenate([found, found], axis=1)
    side = lax.broadcasted_iota(jnp.int32, (SEGS, 128), 1) // 64
    parity = lax.broadcasted_iota(jnp.int32, (SEGS, 128), 0) & 1
    found = jnp.where(side == parity, found, 0)
    for o in range(SEGS):
        ids[o] = found[o : o + 1]


def shift_bank(det, shift_ref, bank_ref, bank):
    split = lax.broadcasted_iota(jnp.int32, (2 * QV, 2 * QV), 0)
    split = 2 * (split % QV) + split // QV
    split = jnp.where(split == lax.broadcasted_iota(jnp.int32, (2 * QV, 2 * QV), 1), 1.0, 0.0)
    split = split.astype(BF16)
    k = lax.broadcasted_iota(jnp.int32, (QV, 128), 0) + det * QV
    m = lax.broadcasted_iota(jnp.int32, (8, HALF), 1)
    for b in range(BLOCK):
        shift = shift_ref[b]
        angle = (-2.0 * math.pi / SAMPLES) * ((k * shift) % SAMPLES).astype(F32)
        row_cos, row_sin = jnp.cos(angle)[:, :1], jnp.sin(angle)[:, :1]
        angle = (-2.0 * math.pi / U) * ((m * shift) % U).astype(F32)
        col_cos, col_sin = jnp.cos(angle)[:1], jnp.sin(angle)[:1]
        pairs = bank_ref[b].reshape(2 * QV, HALF)
        parts = jnp.dot(split, pairs, preferred_element_type=F32)
        real, imag = parts[:QV], parts[QV:]
        cosine = row_cos * col_cos - row_sin * col_sin
        sine = row_cos * col_sin + row_sin * col_cos
        bank[b, :, :HALF] = (real * cosine - imag * sine).astype(BF16)
        bank[b, :, HALF:] = (real * sine + imag * cosine).astype(BF16)


PIECES = 16
PIECE = V // PIECES


def filter_kernel(
    start_ref, width_ref, shift_ref, target_ref, bank_ref, strain_ref, psd_hbm, row_hbm, twist_hbm, col_hbm,
    coherent_ref, full_ref, next_ref, after_ref,
    held, dest, rows, ids, arrived, arrived_ids, chosen, total, bank, relay,
    turned, crossed, sums, mine, psd, row, twist, col,
    row_send, row_recv, id_send, id_recv, bank_send, bank_recv, turn_send, turn_recv,
    coh_send, coh_recv, pass_send, pass_recv, piece_send, relay_recv, table_sem, own_sem,
):
    me = lax.axis_index("seg")
    det = lax.axis_index("det")
    core = me % 2
    place = (me % 32) // 2
    barrier = pltpu.get_barrier_semaphore()

    def greet(o, _):
        pl.semaphore_signal(
            barrier, inc=1, device_id={"seg": (me + o) % SEGS}, device_id_type=MESH
        )
        return 0

    lax.fori_loop(1, SEGS, greet, 0)
    for o in range(1, DETS):
        pl.semaphore_signal(
            barrier, inc=1, device_id={"det": (det + o) % DETS}, device_id_type=MESH
        )
    fetches = [
        pltpu.make_async_copy(source, held_at, table_sem.at[i])
        for i, (source, held_at) in enumerate(
            ((row_hbm, row), (twist_hbm.at[det], twist), (col_hbm, col), (psd_hbm, psd))
        )
    ]
    for fetch in fetches:
        fetch.start()
    shift_bank(det, shift_ref, bank_ref, bank)
    own_bank = pltpu.make_async_copy(
        bank.at[det], full_ref.at[pl.ds(det * QV, QV)], own_sem.at[0]
    )
    own_bank.start()
    pl.semaphore_wait(barrier, SEGS + DETS - 2)

    def bank_copy(o):
        other = (det + o) % DETS
        return pltpu.make_async_remote_copy(
            src_ref=bank.at[other],
            dst_ref=full_ref.at[pl.ds(det * QV, QV)],
            send_sem=bank_send.at[o],
            recv_sem=bank_recv.at[o],
            device_id={"det": other},
            device_id_type=MESH,
        )

    for o in (2, 1, 3):
        bank_copy(o).start()

    def row_copy(o):
        return pltpu.make_async_remote_copy(
            src_ref=rows.at[pl.ds(o * CAP, CAP)],
            dst_ref=arrived.at[o, pl.ds(0, CAP)],
            send_sem=row_send.at[o],
            recv_sem=row_recv.at[o],
            device_id={"seg": (me + o) % SEGS},
            device_id_type=MESH,
        )

    def id_copy(o):
        return pltpu.make_async_remote_copy(
            src_ref=ids.at[o],
            dst_ref=arrived_ids.at[o],
            send_sem=id_send.at[o],
            recv_sem=id_recv.at[o],
            device_id={"seg": (me + o) % SEGS},
            device_id_type=MESH,
        )

    held[...] = strain_ref[...].astype(BF16)
    sort_ranks(me, target_ref, dest, ids)
    step = GROUP * CAP

    def send(o, _):
        id_copy(o).start()
        row_copy(o).start()
        return 0

    for g in range(SEGS // GROUP):
        want = lax.broadcasted_iota(jnp.int32, (step, LANES), 0) + g * step
        picks = [
            jnp.where(want == dest[b : b + 1, :], 1.0, 0.0).astype(BF16) for b in range(COUNT)
        ]
        picked = jnp.dot(jnp.concatenate(picks, axis=1), held[...], preferred_element_type=F32)
        rows[g * step : (g + 1) * step] = picked.astype(BF16)
        lax.fori_loop(max(1, g * GROUP), (g + 1) * GROUP, send, 0)
    own_rows = pltpu.make_async_copy(
        rows.at[pl.ds(0, CAP)], arrived.at[0, pl.ds(0, CAP)], own_sem.at[1]
    )
    own_rows.start()
    own_ids = pltpu.make_async_copy(ids.at[0], arrived_ids.at[0], own_sem.at[2])
    own_ids.start()
    arrived[:, CAP:, :] = jnp.zeros((SEGS, 64 - CAP, QU), BF16)

    own_bank.wait()
    for o in range(1, DETS):
        bank_copy(o).wait_recv()

    def whole_pass(source, target, lane, back):
        return pltpu.make_async_remote_copy(
            src_ref=source,
            dst_ref=target,
            send_sem=pass_send.at[lane],
            recv_sem=pass_recv.at[lane],
            device_id={"seg": (me + SEGS - back) % SEGS},
            device_id_type=MESH,
        )

    hot = (me % 32) < 2
    odd = core == 1
    to_next = whole_pass(full_ref, next_ref, 0, 1)
    to_after = whole_pass(full_ref, after_ref, 1, 2)
    onward = pltpu.make_async_remote_copy(
        src_ref=next_ref,
        dst_ref=after_ref,
        send_sem=pass_send.at[2],
        recv_sem=pass_recv.at[1],
        device_id={"seg": (me + SEGS - 1) % SEGS},
        device_id_type=MESH,
    )
    corner = (me // 32) * 32
    far = (corner + SEGS - 1) % SEGS

    def piece_copy(i):
        return pltpu.make_async_remote_copy(
            src_ref=full_ref.at[pl.ds(i * PIECE, PIECE)],
            dst_ref=relay,
            send_sem=piece_send.at[i],
            recv_sem=relay_recv.at[0],
            device_id={"seg": corner + 2 * i + core},
            device_id_type=MESH,
        )

    def last_hop(source, target, lane, at):
        return pltpu.make_async_remote_copy(
            src_ref=source,
            dst_ref=target.at[pl.ds(at * PIECE, PIECE)],
            send_sem=piece_send.at[0],
            recv_sem=pass_recv.at[lane],
            device_id={"seg": far},
            device_id_type=MESH,
        )

    def pieces(i, _):
        piece_copy(i).start()
        return 0

    def pieces_sent(i, _):
        piece_copy(i).wait_send()
        return 0

    @pl.when(jnp.logical_or(odd, jnp.logical_not(hot)))
    def _():
        to_next.start()

    @pl.when(jnp.logical_and(odd, jnp.logical_not(hot)))
    def _():
        to_after.start()

    @pl.when(hot)
    def _():
        lax.fori_loop(1, PIECES, pieces, 0)

    @pl.when(jnp.logical_and(hot, odd))
    def _():
        last_hop(full_ref.at[pl.ds(0, PIECE)], after_ref, 1, 0).start()

    @pl.when(jnp.logical_and(hot, jnp.logical_not(odd)))
    def _():
        last_hop(full_ref.at[pl.ds(0, PIECE)], next_ref, 0, 0).start()

    own_rows.wait()
    own_ids.wait()

    def receive(o, _):
        id_copy(o).wait_recv()
        row_copy(o).wait_recv()
        return 0

    wide = GROUP * 64
    groups = SEGS // GROUP
    for g in range(groups):
        if g == 1:

            @pl.when(jnp.logical_not(hot))
            def _():
                piece_copy(1).wait_recv()

            @pl.when(jnp.logical_and(jnp.logical_not(hot), odd))
            def _():
                last_hop(relay, after_ref, 1, place).start()

            @pl.when(jnp.logical_and(jnp.logical_not(hot), jnp.logical_not(odd)))
            def _():
                last_hop(relay, next_ref, 0, place).start()

        if g == 3:
            to_next.wait_recv()

            @pl.when(odd)
            def _():
                onward.start()

        lax.fori_loop(max(1, g * GROUP), (g + 1) * GROUP, receive, 0)
        for p in range(GROUP // 2):
            o = g * GROUP + 2 * p
            ident = arrived_ids[o] + arrived_ids[o + 1] - 1
            chosen[:, p * 128 : (p + 1) * 128] = jnp.where(
                lax.broadcasted_iota(jnp.int32, (ROWS, 128), 0) == ident, 1.0, 0.0
            ).astype(BF16)
        block = arrived[g * GROUP : (g + 1) * GROUP].reshape(wide, QU)
        part = jnp.dot(chosen[...], block, preferred_element_type=F32)
        if g == 0:
            total[...] = part
        else:
            total[...] += part

    def turn_copy(o, d):
        other = (det + o) % DETS
        return pltpu.make_async_remote_copy(
            src_ref=turned.at[other, d],
            dst_ref=crossed.at[o, d],
            send_sem=turn_send.at[o, d],
            recv_sem=turn_recv.at[o, d],
            device_id={"det": other},
            device_id_type=MESH,
        )

    sample = lax.broadcasted_iota(jnp.int32, (V, QU), 0) * U
    sample = sample + lax.broadcasted_iota(jnp.int32, (V, QU), 1) + det * QU
    for fetch in fetches:
        fetch.wait()
    for d in range(DETECTORS):
        begin = start_ref[0, d]
        end = begin + width_ref[0, d]
        inside = (sample >= begin) & (sample < end)
        gated = jnp.where(inside, 0.0, total[d * V : (d + 1) * V]).astype(BF16)
        folded = jnp.dot(row[...], gated, preferred_element_type=F32)
        real, imag = folded[:V], folded[V:]
        cosine, sine = twist[0], twist[1]
        first = (real * cosine - imag * sine).astype(BF16)
        second = (real * sine + imag * cosine).astype(BF16)
        for q in range(DETS):
            turned[q, d, :, :QU] = first[q * QV : (q + 1) * QV]
            turned[q, d, :, QU:] = second[q * QV : (q + 1) * QV]
        for o in (2, 1, 3):
            turn_copy(o, d).start()
    for d in range(DETECTORS):
        part = jnp.dot(turned[det, d], col[det], preferred_element_type=F32)
        for o in (1, 3, 2):
            turn_copy(o, d).wait_recv()
            part = part + jnp.dot(
                crossed[o, d], col[(det + DETS - o) % DETS], preferred_element_type=F32
            )
        for half in range(2):
            cols = slice(half * HALF, (half + 1) * HALF)
            value = psd[d] * part[:, cols]
            if d == 0:
                sums[:, cols] = value
            elif d < DETECTORS - 1:
                sums[:, cols] += value
            else:
                mine[:, cols] = (sums[:, cols] + value).astype(BF16)

    def coherent_copy(o):
        return pltpu.make_async_remote_copy(
            src_ref=mine,
            dst_ref=coherent_ref.at[pl.ds(det * QV, QV)],
            send_sem=coh_send.at[o],
            recv_sem=coh_recv.at[o],
            device_id={"det": (det + o) % DETS},
            device_id_type=MESH,
        )

    for o in (2, 1, 3):
        coherent_copy(o).start()
    keep = pltpu.make_async_copy(mine, coherent_ref.at[pl.ds(det * QV, QV)], own_sem.at[3])
    keep.start()

    to_after.wait_recv()

    @pl.when(jnp.logical_or(odd, jnp.logical_not(hot)))
    def _():
        to_next.wait_send()

    @pl.when(jnp.logical_and(odd, jnp.logical_not(hot)))
    def _():
        to_after.wait_send()

    @pl.when(hot)
    def _():
        lax.fori_loop(1, PIECES, pieces_sent, 0)

    last_hop(relay, next_ref, 0, place).wait_send()

    @pl.when(odd)
    def _():
        onward.wait_send()

    def sent(o, _):
        id_copy(o).wait_send()
        row_copy(o).wait_send()
        return 0

    lax.fori_loop(1, SEGS, sent, 0)
    for o in range(1, DETS):
        bank_copy(o).wait_send()
        for d in range(DETECTORS):
            turn_copy(o, d).wait_send()
    for o in (1, 3, 2):
        coherent_copy(o).wait()
    keep.wait()


def filtered(start, width, shift, target, bank, strain, psd, row, twist, col):
    whole = jax.ShapeDtypeStruct((V, U), BF16)
    dma = pltpu.SemaphoreType.DMA
    return pl.pallas_call(
        filter_kernel,
        out_shape=(whole,) * 4,
        in_specs=[SM, SM, SM, VM, VM, VM, HB, HB, HB, HB],
        out_specs=(HB,) * 4,
        scratch_shapes=[
            pltpu.VMEM((SLOTS, QU), BF16),
            pltpu.VMEM((16, LANES), jnp.int32),
            pltpu.VMEM((SLOTS, QU), BF16),
            pltpu.VMEM((SEGS, 1, 128), jnp.int32),
            pltpu.VMEM((SEGS, 64, QU), BF16),
            pltpu.VMEM((SEGS, 1, 128), jnp.int32),
            pltpu.VMEM((ROWS, GROUP * 64), BF16),
            pltpu.VMEM((ROWS, QU), F32),
            pltpu.VMEM((BLOCK, QV, U), BF16),
            pltpu.VMEM((PIECE, U), BF16),
            pltpu.VMEM((DETS, DETECTORS, QV, 2 * QU), BF16),
            pltpu.VMEM((DETS, DETECTORS, QV, 2 * QU), BF16),
            pltpu.VMEM((QV, U), F32),
            pltpu.VMEM((QV, U), BF16),
            pltpu.VMEM((DETECTORS, QV, HALF), F32),
            pltpu.VMEM((2 * V, V), BF16),
            pltpu.VMEM((2, V, QU), F32),
            pltpu.VMEM((DETS, 2 * QU, U), BF16),
            dma((SEGS,)), dma((SEGS,)), dma((SEGS,)), dma((SEGS,)),
            dma((DETS,)), dma((DETS,)),
            dma((DETS, DETECTORS)), dma((DETS, DETECTORS)),
            dma((DETS,)), dma((DETS,)),
            dma((3,)), dma((2,)), dma((PIECES,)), dma((1,)), dma((4,)), dma((4,)),
        ],
        compiler_params=pltpu.CompilerParams(
            vmem_limit_bytes=LIMIT, collective_id=0, has_side_effects=True
        ),
        cost_estimate=pl.CostEstimate(
            flops=12_000_000_000, bytes_accessed=16_000_000, transcendentals=0
        ),
        name="filtered",
    )(start, width, shift, target, bank, strain, psd, row, twist, col)


def inverse_kernel(
    coherent_ref, first_ref, second_ref, third_ref, back_ref, untwist_ref, last_ref, out_ref, partial
):
    real, imag = coherent_ref[:, :HALF].astype(F32), coherent_ref[:, HALF:].astype(F32)
    for r, bank_ref in enumerate((first_ref, second_ref, third_ref)):
        other_real = bank_ref[:, :HALF].astype(F32)
        other_imag = bank_ref[:, HALF:].astype(F32)
        product = jnp.concatenate(
            [
                (real * other_real + imag * other_imag).astype(BF16),
                (imag * other_real - real * other_imag).astype(BF16),
            ],
            axis=1,
        )
        series = jnp.dot(product, back_ref[...], preferred_element_type=F32)
        cosine, sine = untwist_ref[0], untwist_ref[1]
        partial[:V] = (series[:, :U] * cosine - series[:, U:] * sine).astype(BF16)
        partial[V:] = (series[:, :U] * sine + series[:, U:] * cosine).astype(BF16)
        out = jnp.dot(last_ref[...], partial[...], preferred_element_type=F32).astype(BF16)
        out_ref[0, 0, r] = out.reshape(V // 2, 2, U)


def inverse_steps(coherent, banks, back, untwist, last):
    return pl.pallas_call(
        inverse_kernel,
        out_shape=jax.ShapeDtypeStruct((1, 1, STEPS, V // 2, 2, U), BF16),
        in_specs=[VM] * 7,
        out_specs=VM,
        scratch_shapes=[pltpu.VMEM((2 * V, U), BF16)],
        compiler_params=pltpu.CompilerParams(vmem_limit_bytes=LIMIT),
        name="inverse_steps",
    )(coherent, *banks, back, untwist, last)


def body(strain, row_target, gate_start, gate_width, inverse_psd, templates, template_shift):
    row, twist, col, back, untwist, last = (jnp.asarray(t) for t in tables())
    coherent, *banks = filtered(
        gate_start,
        gate_width,
        template_shift,
        row_target.reshape(COUNT, LANES),
        templates,
        strain,
        inverse_psd,
        row,
        twist,
        col,
    )
    return inverse_steps(coherent, banks, back, untwist, last)


def solution(mesh):
    in_specs = (
        P("seg", "det"),
        P("seg"),
        P("seg", None),
        P("seg", None),
        P(None, "det", None),
        P("seg", "det", None, None),
        P("seg"),
    )
    out_specs = P("seg", "det", None, None, None, None)
    return jax.shard_map(body, mesh=mesh, in_specs=in_specs, out_specs=out_specs, check_vma=False)
```

time: 276 us -> 185 us (0.67)
  the two profiles are of different devices: /device:TPU:1 before, /device:TPU:56 now
where the time goes in v2:
time: 185 us
  Pallas kernels  184 us (99%)
    pallas_call x1, Pallas kernels, filtered(): pl.pallas_call(filter_kernel, out_shape=(whole,) * 4, in_specs=[SM, SM, S...  166 us
    pallas_call x1, Pallas kernels, inverse_steps(): pl.pallas_call(inverse_kernel, out_shape=jax.ShapeDtypeStruct((1, 1, STEP...  18.1 us

profile of v2, /device:TPU:56, one launch (start us, length us, event | category | flops | bytes accessed | tf_op | source)
XLA Modules:
  0.0 185.3 jit_solution(5936602441279970151)
XLA Ops:
  0.0 1.3 reshape.3.target_ref
  1.3 165.9 %filtered.1 = (bf16[512,1024]{1,0:T(8,128)(2,1)}, bf16[512,1024]{1,0:T(8,128)(2,1)}, bf16[512,1024]{1,0:T(8,128)(2,1)}, bf16[512,1024]{1,0:T(8,128)(2,1)}) custom-call(s32[1,3]{1,0:T(1,128)} %start_ref.1, s32[1,3]{1,0:T(1,128)} %width_ref.1, s32[4]{0:T(128)} %shift_ref.1, s32[12,256]{1,0:T(8,128)} %reshape.3.target_ref, bf16[4,128,2,512]{3,2,1,0:T(2,128)(2,1)} %bank_ref.1, ...), custom_call_target="tpu_custom_call" | custom-call | flops 12000000000 | bytes 16000000 | tf_op jit(solution)/shard_map/filtered/pallas_call | solution.py:449
  167.2 18.1 %inverse_steps.1 = bf16[1,1,3,256,2,1024]{5,4,3,2,1,0:T(2,128)(2,1)} custom-call(bf16[512,1024]{1,0:T(8,128)(2,1)} %get-tuple-element.9.coherent_ref, bf16[512,1024]{1,0:T(8,128)(2,1)} %get-tuple-element.10.first_ref, bf16[512,1024]{1,0:T(8,128)(2,1)} %get-tuple-element.11.second_ref, bf16[512,1024]{1,0:T(8,128)(2,1)} %get-tuple-element.12.third_ref, ...), custom_call_target="tpu_custom_call" | custom-call | tf_op jit(solution)/shard_map/inverse_steps/pallas_call | solution.py:512

commit v3 on v2

--- a/solution.py
+++ b/solution.py
@@ -23,6 +23,9 @@
 QV = V // DETS
 ROWS = DETECTORS * V
 HALF = U // 2
+SHARE = V // 8
+PLACES = (0, 2, 3, 1)
+MIRROR = 32
 MESH = pl.DeviceIdType.MESH
 F32 = jnp.float32
 BF16 = jnp.bfloat16
@@ -42,14 +45,34 @@
 def tables():
     v, u, m = np.arange(V), np.arange(U), np.arange(HALF)
     bf = np.dtype(jnp.bfloat16)
-    c, s = angles(v, v, V, -1.0)
+    c, s = angles(v[: V // 2], v, V, -1.0)
+    s[0] = np.where(v % 2 == 0, 1.0, -1.0)
     row = (np.concatenate([c, s], 0) / math.sqrt(V)).astype(bf)
-    twist = np.stack([*angles(v, u, SAMPLES, -1.0)])
-    twist = twist.reshape(2, V, DETS, QU).transpose(2, 0, 1, 3).astype(np.float32)
+    twist = np.stack([*angles(v[: V // 2], u, SAMPLES, -1.0)])
+    twist = twist.reshape(2, V // 2, DETS, QU).transpose(2, 0, 1, 3).astype(np.float32)
+    edge = np.stack([*angles(v[V // 2 : V // 2 + 1], u, SAMPLES, -1.0)])
+    edge = edge.reshape(2, 1, DETS, QU).transpose(2, 1, 0, 3).reshape(DETS, 1, 2 * QU)
+    edge = np.tile(edge, (1, 8, 1)).astype(np.float32)
+
+    def by_source(real_rows, imag_rows):
+        both = np.stack([real_rows, imag_rows]) / math.sqrt(U)
+        both = both.reshape(2, DETS, QU, U).transpose(1, 0, 2, 3)
+        return both.reshape(DETS, 2 * QU, U).astype(bf)
+
     c, s = angles(u, m, U, -1.0)
-    col = np.stack([np.concatenate([c, s], 1), np.concatenate([-s, c], 1)])
-    col = (col / math.sqrt(U)).reshape(2, DETS, QU, U).transpose(1, 0, 2, 3)
-    col = col.reshape(DETS, 2 * QU, U).astype(bf)
+    direct = by_source(np.concatenate([c, s], 1), np.concatenate([-s, c], 1))
+    c, s = angles(u, m + 1, U, -1.0)
+    mirrored = by_source(np.concatenate([c, s], 1), np.concatenate([s, -c], 1))
+    col = np.stack([direct, mirrored])
+    place = np.zeros(V, np.int64)
+    for k in range(V):
+        low = k if k < V // 2 else (V - k) % (V // 2)
+        device = PLACES.index(low // SHARE)
+        if k < V // 2:
+            place[k] = device * QV + low % SHARE
+        else:
+            place[k] = device * QV + QV - 1 - low % SHARE
+    perm = (place[:, None] == v[None, :]).astype(bf)
     c, s = angles(m, u, U, 1.0)
     back = np.concatenate([np.concatenate([c, s], 1), np.concatenate([-s, c], 1)], 0)
     back = (back / math.sqrt(U)).astype(bf)
@@ -57,7 +80,7 @@
     c, s = angles(np.arange(V // 4, 3 * V // 4), v, V, 1.0)
     last = np.stack([np.concatenate([c, -s], 1), np.concatenate([s, c], 1)], 1)
     last = (last / math.sqrt(V)).reshape(V, 2 * V).astype(bf)
-    return row, twist, col, back, untwist, last
+    return row, twist, edge, col, perm, back, untwist, last
 
 
 GROUP = 16
@@ -75,7 +98,7 @@
     low = jnp.zeros((SEGS, SEGS), F32)
     spread = (((1,), (1,)), ((), ()))
     for b in range(COUNT):
-        t = target_ref[b : b + 1, :]
+        t = target_ref[b * LANES : (b + 1) * LANES].reshape(1, LANES)
         owner = ((t >> 9) * 43691) >> 17
         local = t - owner * ROWS
         owner = jnp.where(t >= 0, (owner + SEGS - me) & (SEGS - 1), SEGS)
@@ -125,12 +148,12 @@
 
 
 def filter_kernel(
-    start_ref, width_ref, shift_ref, target_ref, bank_ref, strain_ref, psd_hbm, row_hbm, twist_hbm, col_hbm,
+    start_ref, width_ref, shift_ref, target_ref, edge_ref, bank_ref, strain_ref, psd_hbm, row_hbm, twist_hbm, col_hbm,
     coherent_ref, full_ref, next_ref, after_ref,
     held, dest, rows, ids, arrived, arrived_ids, chosen, total, bank, relay,
-    turned, crossed, sums, mine, psd, row, twist, col,
+    turned, crossed, spec, mine, psd_low, psd_high, row, twist, col,
     row_send, row_recv, id_send, id_recv, bank_send, bank_recv, turn_send, turn_recv,
-    coh_send, coh_recv, pass_send, pass_recv, piece_send, relay_recv, table_sem, own_sem,
+    coh_send, coh_recv, pass_send, pass_recv, piece_send, relay_recv, psd_send, psd_recv, table_sem, own_sem,
 ):
     me = lax.axis_index("seg")
     det = lax.axis_index("det")
@@ -149,10 +172,12 @@
         pl.semaphore_signal(
             barrier, inc=1, device_id={"det": (det + o) % DETS}, device_id_type=MESH
         )
+    across = {"seg": (me + MIRROR) % SEGS, "det": DETS - 1 - det}
+    pl.semaphore_signal(barrier, inc=1, device_id=across, device_id_type=MESH)
     fetches = [
         pltpu.make_async_copy(source, held_at, table_sem.at[i])
         for i, (source, held_at) in enumerate(
-            ((row_hbm, row), (twist_hbm.at[det], twist), (col_hbm, col), (psd_hbm, psd))
+            ((row_hbm, row), (twist_hbm.at[det], twist), (col_hbm, col))
         )
     ]
     for fetch in fetches:
@@ -162,7 +187,7 @@
         bank.at[det], full_ref.at[pl.ds(det * QV, QV)], own_sem.at[0]
     )
     own_bank.start()
-    pl.semaphore_wait(barrier, SEGS + DETS - 2)
+    pl.semaphore_wait(barrier, SEGS + DETS - 1)
 
     def bank_copy(o):
         other = (det + o) % DETS
@@ -177,6 +202,42 @@
 
     for o in (2, 1, 3):
         bank_copy(o).start()
+
+    upper_det = det >= DETS // 2
+
+    def psd_copy(target, lane):
+        return pltpu.make_async_remote_copy(
+            src_ref=psd_hbm.at[:, pl.ds(SHARE, SHARE)],
+            dst_ref=target,
+            send_sem=psd_send.at[0],
+            recv_sem=psd_recv.at[lane],
+            device_id=across,
+            device_id_type=MESH,
+        )
+
+    to_low = psd_copy(psd_low, 0)
+    to_high = psd_copy(psd_high.at[:, pl.ds(0, SHARE)], 0)
+    to_rest = pltpu.make_async_remote_copy(
+        src_ref=psd_hbm.at[:, pl.ds(0, 8)],
+        dst_ref=psd_high.at[:, pl.ds(SHARE, 8)],
+        send_sem=psd_send.at[1],
+        recv_sem=psd_recv.at[1],
+        device_id={"det": (det + 2) % DETS},
+        device_id_type=MESH,
+    )
+    keep_low = pltpu.make_async_copy(psd_hbm.at[:, pl.ds(0, SHARE)], psd_low, own_sem.at[4])
+    keep_high = pltpu.make_async_copy(psd_hbm.at[:, pl.ds(0, SHARE + 8)], psd_high, own_sem.at[4])
+
+    @pl.when(upper_det)
+    def _():
+        to_high.start()
+        to_rest.start()
+        keep_high.start()
+
+    @pl.when(jnp.logical_not(upper_det))
+    def _():
+        to_low.start()
+        keep_low.start()
 
     def row_copy(o):
         return pltpu.make_async_remote_copy(
@@ -311,27 +372,6 @@
     wide = GROUP * 64
     groups = SEGS // GROUP
     for g in range(groups):
-        if g == 1:
-
-            @pl.when(jnp.logical_not(hot))
-            def _():
-                piece_copy(1).wait_recv()
-
-            @pl.when(jnp.logical_and(jnp.logical_not(hot), odd))
-            def _():
-                last_hop(relay, after_ref, 1, place).start()
-
-            @pl.when(jnp.logical_and(jnp.logical_not(hot), jnp.logical_not(odd)))
-            def _():
-                last_hop(relay, next_ref, 0, place).start()
-
-        if g == 3:
-            to_next.wait_recv()
-
-            @pl.when(odd)
-            def _():
-                onward.start()
-
         lax.fori_loop(max(1, g * GROUP), (g + 1) * GROUP, receive, 0)
         for p in range(GROUP // 2):
             o = g * GROUP + 2 * p
@@ -367,31 +407,79 @@
         inside = (sample >= begin) & (sample < end)
         gated = jnp.where(inside, 0.0, total[d * V : (d + 1) * V]).astype(BF16)
         folded = jnp.dot(row[...], gated, preferred_element_type=F32)
-        real, imag = folded[:V], folded[V:]
+        real, imag = folded[: V // 2], folded[V // 2 :]
         cosine, sine = twist[0], twist[1]
         first = (real * cosine - imag * sine).astype(BF16)
         second = (real * sine + imag * cosine).astype(BF16)
         for q in range(DETS):
-            turned[q, d, :, :QU] = first[q * QV : (q + 1) * QV]
-            turned[q, d, :, QU:] = second[q * QV : (q + 1) * QV]
+            at = PLACES[q] * SHARE
+            turned[q, d, :, :QU] = first[at : at + SHARE]
+            turned[q, d, :, QU:] = second[at : at + SHARE]
         for o in (2, 1, 3):
             turn_copy(o, d).start()
-    for d in range(DETECTORS):
-        part = jnp.dot(turned[det, d], col[det], preferred_element_type=F32)
-        for o in (1, 3, 2):
-            turn_copy(o, d).wait_recv()
-            part = part + jnp.dot(
-                crossed[o, d], col[(det + DETS - o) % DETS], preferred_element_type=F32
-            )
-        for half in range(2):
-            cols = slice(half * HALF, (half + 1) * HALF)
-            value = psd[d] * part[:, cols]
-            if d == 0:
-                sums[:, cols] = value
-            elif d < DETECTORS - 1:
-                sums[:, cols] += value
-            else:
-                mine[:, cols] = (sums[:, cols] + value).astype(BF16)
+
+    @pl.when(jnp.logical_not(hot))
+    def _():
+        piece_copy(1).wait_recv()
+
+    @pl.when(jnp.logical_and(jnp.logical_not(hot), odd))
+    def _():
+        last_hop(relay, after_ref, 1, place).start()
+
+    @pl.when(jnp.logical_and(jnp.logical_not(hot), jnp.logical_not(odd)))
+    def _():
+        last_hop(relay, next_ref, 0, place).start()
+
+    high = DETECTORS * SHARE
+    row_at = lax.broadcasted_iota(jnp.int32, (high, high), 0)
+    col_at = lax.broadcasted_iota(jnp.int32, (high, high), 1)
+    flip = (row_at // SHARE == col_at // SHARE) & (row_at % SHARE + col_at % SHARE == SHARE - 1)
+    flip = jnp.where(flip, 1.0, 0.0).astype(BF16)
+    packed = lax.broadcasted_iota(jnp.int32, (high, 2 * QU), 0) % SHARE + det == 0
+    imag_side = lax.broadcasted_iota(jnp.int32, (high, 2 * QU), 1) >= QU
+    for o in (0, 1, 3, 2):
+        source = (det + DETS - o) % DETS
+        if o == 0:
+            came = turned[det]
+        else:
+            for d in range(DETECTORS):
+                turn_copy(o, d).wait_recv()
+            came = crossed[o]
+        came = came.reshape(high, 2 * QU)
+        wide_came = came.astype(F32)
+        direct = jnp.where(packed & imag_side, 0.0, wide_came).astype(BF16)
+        twin = wide_came[:, QU:]
+        twin = jnp.concatenate([twin, twin], axis=1) * edge_ref[source][:1]
+        mirrored = jnp.where(packed, twin, wide_came).astype(BF16)
+        mirrored = jnp.dot(flip, mirrored, preferred_element_type=F32).astype(BF16)
+        part = jnp.dot(direct, col[0, source], preferred_element_type=F32)
+        other = jnp.dot(mirrored, col[1, source], preferred_element_type=F32)
+        if o == 0:
+            spec[0], spec[1] = part, other
+        else:
+            spec[0] += part
+            spec[1] += other
+
+    @pl.when(upper_det)
+    def _():
+        to_low.wait_recv()
+        keep_high.wait()
+
+    @pl.when(jnp.logical_not(upper_det))
+    def _():
+        to_high.wait_recv()
+        to_rest.wait_recv()
+        keep_low.wait()
+
+    for half in range(2):
+        cols = slice(half * HALF, (half + 1) * HALF)
+        direct, mirrored = 0.0, 0.0
+        for d in range(DETECTORS):
+            rows_of = slice(d * SHARE, (d + 1) * SHARE)
+            direct = direct + psd_low[d] * spec[0, rows_of, cols]
+            mirrored = mirrored + psd_high[d, 1 : SHARE + 1] * spec[1, rows_of, cols]
+        mine[:SHARE, cols] = direct.astype(BF16)
+        mine[SHARE:, cols] = mirrored.astype(BF16)
 
     def coherent_copy(o):
         return pltpu.make_async_remote_copy(
@@ -408,7 +496,23 @@
     keep = pltpu.make_async_copy(mine, coherent_ref.at[pl.ds(det * QV, QV)], own_sem.at[3])
     keep.start()
 
+    to_next.wait_recv()
+
+    @pl.when(odd)
+    def _():
+        onward.start()
+
     to_after.wait_recv()
+
+    @pl.when(upper_det)
+    def _():
+        to_high.wait_send()
+        to_rest.wait_send()
+
+    @pl.when(jnp.logical_not(upper_det))
+    def _():
+        to_low.wait_send()
+
 
     @pl.when(jnp.logical_or(odd, jnp.logical_not(hot)))
     def _():
@@ -443,13 +547,13 @@
     keep.wait()
 
 
-def filtered(start, width, shift, target, bank, strain, psd, row, twist, col):
+def filtered(start, width, shift, target, edge, bank, strain, psd, row, twist, col):
     whole = jax.ShapeDtypeStruct((V, U), BF16)
     dma = pltpu.SemaphoreType.DMA
     return pl.pallas_call(
         filter_kernel,
         out_shape=(whole,) * 4,
-        in_specs=[SM, SM, SM, VM, VM, VM, HB, HB, HB, HB],
+        in_specs=[SM, SM, SM, VM, VM, VM, VM, HB, HB, HB, HB],
         out_specs=(HB,) * 4,
         scratch_shapes=[
             pltpu.VMEM((SLOTS, QU), BF16),
@@ -462,19 +566,20 @@
             pltpu.VMEM((ROWS, QU), F32),
             pltpu.VMEM((BLOCK, QV, U), BF16),
             pltpu.VMEM((PIECE, U), BF16),
-            pltpu.VMEM((DETS, DETECTORS, QV, 2 * QU), BF16),
-            pltpu.VMEM((DETS, DETECTORS, QV, 2 * QU), BF16),
-            pltpu.VMEM((QV, U), F32),
+            pltpu.VMEM((DETS, DETECTORS, SHARE, 2 * QU), BF16),
+            pltpu.VMEM((DETS, DETECTORS, SHARE, 2 * QU), BF16),
+            pltpu.VMEM((2, DETECTORS * SHARE, U), F32),
             pltpu.VMEM((QV, U), BF16),
-            pltpu.VMEM((DETECTORS, QV, HALF), F32),
-            pltpu.VMEM((2 * V, V), BF16),
-            pltpu.VMEM((2, V, QU), F32),
-            pltpu.VMEM((DETS, 2 * QU, U), BF16),
+            pltpu.VMEM((DETECTORS, SHARE, HALF), F32),
+            pltpu.VMEM((DETECTORS, SHARE + 8, HALF), F32),
+            pltpu.VMEM((V, V), BF16),
+            pltpu.VMEM((2, V // 2, QU), F32),
+            pltpu.VMEM((2, DETS, 2 * QU, U), BF16),
             dma((SEGS,)), dma((SEGS,)), dma((SEGS,)), dma((SEGS,)),
             dma((DETS,)), dma((DETS,)),
             dma((DETS, DETECTORS)), dma((DETS, DETECTORS)),
             dma((DETS,)), dma((DETS,)),
-            dma((3,)), dma((2,)), dma((PIECES,)), dma((1,)), dma((4,)), dma((4,)),
+            dma((3,)), dma((2,)), dma((PIECES,)), dma((1,)), dma((2,)), dma((2,)), dma((3,)), dma((5,)),
         ],
         compiler_params=pltpu.CompilerParams(
             vmem_limit_bytes=LIMIT, collective_id=0, has_side_effects=True
@@ -483,50 +588,96 @@
             flops=12_000_000_000, bytes_accessed=16_000_000, transcendentals=0
         ),
         name="filtered",
-    )(start, width, shift, target, bank, strain, psd, row, twist, col)
+    )(start, width, shift, target, edge, bank, strain, psd, row, twist, col)
+
+
+CHUNK = 256
 
 
 def inverse_kernel(
-    coherent_ref, first_ref, second_ref, third_ref, back_ref, untwist_ref, last_ref, out_ref, partial
+    coherent_hbm, first_hbm, second_hbm, third_hbm, perm_hbm, back_hbm, untwist_hbm, last_hbm, out_hbm,
+    coherent, banks, perm, back, untwist, last, products, partials, outs, load_sem, out_sem,
 ):
-    real, imag = coherent_ref[:, :HALF].astype(F32), coherent_ref[:, HALF:].astype(F32)
-    for r, bank_ref in enumerate((first_ref, second_ref, third_ref)):
-        other_real = bank_ref[:, :HALF].astype(F32)
-        other_imag = bank_ref[:, HALF:].astype(F32)
-        product = jnp.concatenate(
-            [
-                (real * other_real + imag * other_imag).astype(BF16),
-                (imag * other_real - real * other_imag).astype(BF16),
-            ],
-            axis=1,
-        )
-        series = jnp.dot(product, back_ref[...], preferred_element_type=F32)
-        cosine, sine = untwist_ref[0], untwist_ref[1]
-        partial[:V] = (series[:, :U] * cosine - series[:, U:] * sine).astype(BF16)
-        partial[V:] = (series[:, :U] * sine + series[:, U:] * cosine).astype(BF16)
-        out = jnp.dot(last_ref[...], partial[...], preferred_element_type=F32).astype(BF16)
-        out_ref[0, 0, r] = out.reshape(V // 2, 2, U)
-
-
-def inverse_steps(coherent, banks, back, untwist, last):
+    loads = [
+        pltpu.make_async_copy(source, target, load_sem.at[i])
+        for i, (source, target) in enumerate(
+            (
+                (coherent_hbm, coherent),
+                (perm_hbm, perm),
+                (first_hbm, banks.at[0]),
+                (back_hbm, back),
+                (untwist_hbm, untwist),
+                (last_hbm, last),
+                (second_hbm, banks.at[1]),
+                (third_hbm, banks.at[2]),
+            )
+        )
+    ]
+    for load in loads:
+        load.start()
+    loads[0].wait()
+    loads[1].wait()
+    whole = jnp.dot(perm[...], coherent[...], preferred_element_type=F32).astype(BF16)
+    coherent[...] = whole
+    outgoing = []
+    for r in range(STEPS):
+        loads[(2, 6, 7)[r]].wait()
+        real, imag = coherent[:, :HALF].astype(F32), coherent[:, HALF:].astype(F32)
+        other_real = banks[r, :, :HALF].astype(F32)
+        other_imag = banks[r, :, HALF:].astype(F32)
+        products[r, :, :HALF] = (real * other_real + imag * other_imag).astype(BF16)
+        products[r, :, HALF:] = (imag * other_real - real * other_imag).astype(BF16)
+        if r == 0:
+            for i in (3, 4, 5):
+                loads[i].wait()
+        for c in range(U // CHUNK):
+            lanes = slice(c * CHUNK, (c + 1) * CHUNK)
+            upper = slice(U + c * CHUNK, U + (c + 1) * CHUNK)
+            first = jnp.dot(products[r], back[:, lanes], preferred_element_type=F32)
+            second = jnp.dot(products[r], back[:, upper], preferred_element_type=F32)
+            cosine, sine = untwist[0, :, lanes], untwist[1, :, lanes]
+            partials[c % 2, :V] = (first * cosine - second * sine).astype(BF16)
+            partials[c % 2, V:] = (first * sine + second * cosine).astype(BF16)
+            made = jnp.dot(last[...], partials[c % 2], preferred_element_type=F32).astype(BF16)
+            outs[r, :, :, lanes] = made.reshape(V // 2, 2, CHUNK)
+        outgoing.append(pltpu.make_async_copy(outs.at[r], out_hbm.at[0, 0, r], out_sem.at[r]))
+        outgoing[r].start()
+    for leaving in outgoing:
+        leaving.wait()
+
+
+def inverse_steps(coherent, banks, perm, back, untwist, last):
     return pl.pallas_call(
         inverse_kernel,
         out_shape=jax.ShapeDtypeStruct((1, 1, STEPS, V // 2, 2, U), BF16),
-        in_specs=[VM] * 7,
-        out_specs=VM,
-        scratch_shapes=[pltpu.VMEM((2 * V, U), BF16)],
+        in_specs=[HB] * 8,
+        out_specs=HB,
+        scratch_shapes=[
+            pltpu.VMEM((V, U), BF16),
+            pltpu.VMEM((STEPS, V, U), BF16),
+            pltpu.VMEM((V, V), BF16),
+            pltpu.VMEM((U, 2 * U), BF16),
+            pltpu.VMEM((2, V, U), F32),
+            pltpu.VMEM((V, 2 * V), BF16),
+            pltpu.VMEM((STEPS, V, U), BF16),
+            pltpu.VMEM((2, 2 * V, CHUNK), BF16),
+            pltpu.VMEM((STEPS, V // 2, 2, U), BF16),
+            pltpu.SemaphoreType.DMA((8,)),
+            pltpu.SemaphoreType.DMA((STEPS,)),
+        ],
         compiler_params=pltpu.CompilerParams(vmem_limit_bytes=LIMIT),
         name="inverse_steps",
-    )(coherent, *banks, back, untwist, last)
+    )(coherent, *banks, perm, back, untwist, last)
 
 
 def body(strain, row_target, gate_start, gate_width, inverse_psd, templates, template_shift):
-    row, twist, col, back, untwist, last = (jnp.asarray(t) for t in tables())
+    row, twist, edge, col, perm, back, untwist, last = (jnp.asarray(t) for t in tables())
     coherent, *banks = filtered(
         gate_start,
         gate_width,
         template_shift,
-        row_target.reshape(COUNT, LANES),
+        row_target,
+        edge,
         templates,
         strain,
         inverse_psd,
@@ -534,7 +685,7 @@
         twist,
         col,
     )
-    return inverse_steps(coherent, banks, back, untwist, last)
+    return inverse_steps(coherent, banks, perm, back, untwist, last)
 
 
 def solution(mesh):

time: 185 us -> 164 us (0.89)
  the two profiles are of different devices: /device:TPU:56 before, /device:TPU:95 now
where the time goes in v3:
time: 164 us
  Pallas kernels  164 us (100%)
    pallas_call x1, Pallas kernels, filtered(): pl.pallas_call(filter_kernel, out_shape=(whole,) * 4, in_specs=[SM, SM, S...  144 us
    pallas_call x1, Pallas kernels, inverse_steps(): pl.pallas_call(inverse_kernel, out_shape=jax.ShapeDtypeStruct((1, 1, STEP...  19.9 us

profile of v3, /device:TPU:95, one launch (start us, length us, event | category | flops | bytes accessed | tf_op | source)
XLA Modules:
  0.0 164.2 jit_solution(18190745286537666389)
XLA Ops:
  0.0 144.1 %filtered.1 = (bf16[512,1024]{1,0:T(8,128)(2,1)}, bf16[512,1024]{1,0:T(8,128)(2,1)}, bf16[512,1024]{1,0:T(8,128)(2,1)}, bf16[512,1024]{1,0:T(8,128)(2,1)}) custom-call(s32[1,3]{1,0:T(1,128)} %start_ref.1, s32[1,3]{1,0:T(1,128)} %width_ref.1, s32[4]{0:T(128)} %shift_ref.1, s32[3072]{0:T(1024)} %target_ref.1, f32[4,8,512]{2,1,0:T(8,128)} %constant.18.clone.edge_ref, ...), custom_call_target="tpu_custom_call" | custom-call | flops 12000000000 | bytes 16000000 | tf_op jit(solution)/shard_map/filtered/pallas_call | solution.py:553
  144.1 19.9 %inverse_steps.1 = bf16[1,1,3,256,2,1024]{5,4,3,2,1,0:T(2,128)(2,1)} custom-call(bf16[512,1024]{1,0:T(8,128)(2,1)} %get-tuple-element.9.coherent_hbm, bf16[512,1024]{1,0:T(8,128)(2,1)} %get-tuple-element.10.first_hbm, bf16[512,1024]{1,0:T(8,128)(2,1)} %get-tuple-element.11.second_hbm, bf16[512,1024]{1,0:T(8,128)(2,1)} %get-tuple-element.12.third_hbm, ...), custom_call_target="tpu_custom_call" | custom-call | tf_op jit(solution)/shard_map/inverse_steps/pallas_call | solution.py:650

commit v4 on v3

--- a/solution.py
+++ b/solution.py
@@ -64,23 +64,22 @@
     c, s = angles(u, m + 1, U, -1.0)
     mirrored = by_source(np.concatenate([c, s], 1), np.concatenate([s, -c], 1))
     col = np.stack([direct, mirrored])
-    place = np.zeros(V, np.int64)
-    for k in range(V):
-        low = k if k < V // 2 else (V - k) % (V // 2)
-        device = PLACES.index(low // SHARE)
-        if k < V // 2:
-            place[k] = device * QV + low % SHARE
-        else:
-            place[k] = device * QV + QV - 1 - low % SHARE
-    perm = (place[:, None] == v[None, :]).astype(bf)
+    order = np.concatenate(
+        [
+            np.concatenate([p * SHARE + half, V - p * SHARE - half[::-1]])
+            for p, half in ((p, np.arange(SHARE)) for p in PLACES)
+        ]
+    )
+    order[QV - 1] = V // 2
     c, s = angles(m, u, U, 1.0)
     back = np.concatenate([np.concatenate([c, s], 1), np.concatenate([-s, c], 1)], 0)
     back = (back / math.sqrt(U)).astype(bf)
-    untwist = np.stack([*angles(v, u, SAMPLES, 1.0)]).astype(np.float32)
-    c, s = angles(np.arange(V // 4, 3 * V // 4), v, V, 1.0)
+    untwist = np.stack([*angles(order, u, SAMPLES, 1.0)]).astype(np.float32)
+    untwist = untwist.reshape(2, DETS, QV, U).transpose(1, 0, 2, 3)
+    c, s = angles(np.arange(V // 4, 3 * V // 4), order, V, 1.0)
     last = np.stack([np.concatenate([c, -s], 1), np.concatenate([s, c], 1)], 1)
     last = (last / math.sqrt(V)).reshape(V, 2 * V).astype(bf)
-    return row, twist, edge, col, perm, back, untwist, last
+    return row, twist, edge, col, back, untwist, last
 
 
 GROUP = 16
@@ -121,26 +120,28 @@
         ids[o] = found[o : o + 1]
 
 
-def shift_bank(det, shift_ref, bank_ref, bank):
-    split = lax.broadcasted_iota(jnp.int32, (2 * QV, 2 * QV), 0)
-    split = 2 * (split % QV) + split // QV
-    split = jnp.where(split == lax.broadcasted_iota(jnp.int32, (2 * QV, 2 * QV), 1), 1.0, 0.0)
-    split = split.astype(BF16)
-    k = lax.broadcasted_iota(jnp.int32, (QV, 128), 0) + det * QV
+def shift_bank(shift, raw, bank):
+    at = lax.broadcasted_iota(jnp.int32, (V, 128), 0)
+    block, inner = at // QV, at % QV
+    base = jnp.where(block == 0, 0, jnp.where(block == 3, SHARE, block * SHARE + SHARE))
+    k = jnp.where(inner < SHARE, base + inner, V - base - (QV - 1) + inner)
+    k = jnp.where(at == QV - 1, V // 2, k)
+    lane = lax.broadcasted_iota(jnp.int32, (V, 2 * V), 1)
+    pairs = raw[...].reshape(2 * V, HALF)
+    parts = []
+    for part in range(2):
+        pick = jnp.where(lane == 2 * k[:, :1] + part, 1.0, 0.0).astype(BF16)
+        parts.append(jnp.dot(pick, pairs, preferred_element_type=F32))
+    real, imag = parts
     m = lax.broadcasted_iota(jnp.int32, (8, HALF), 1)
-    for b in range(BLOCK):
-        shift = shift_ref[b]
-        angle = (-2.0 * math.pi / SAMPLES) * ((k * shift) % SAMPLES).astype(F32)
-        row_cos, row_sin = jnp.cos(angle)[:, :1], jnp.sin(angle)[:, :1]
-        angle = (-2.0 * math.pi / U) * ((m * shift) % U).astype(F32)
-        col_cos, col_sin = jnp.cos(angle)[:1], jnp.sin(angle)[:1]
-        pairs = bank_ref[b].reshape(2 * QV, HALF)
-        parts = jnp.dot(split, pairs, preferred_element_type=F32)
-        real, imag = parts[:QV], parts[QV:]
-        cosine = row_cos * col_cos - row_sin * col_sin
-        sine = row_cos * col_sin + row_sin * col_cos
-        bank[b, :, :HALF] = (real * cosine - imag * sine).astype(BF16)
-        bank[b, :, HALF:] = (real * sine + imag * cosine).astype(BF16)
+    angle = (-2.0 * math.pi / SAMPLES) * ((k * shift) % SAMPLES).astype(F32)
+    row_cos, row_sin = jnp.cos(angle)[:, :1], jnp.sin(angle)[:, :1]
+    angle = (-2.0 * math.pi / U) * ((m * shift) % U).astype(F32)
+    col_cos, col_sin = jnp.cos(angle)[:1], jnp.sin(angle)[:1]
+    cosine = row_cos * col_cos - row_sin * col_sin
+    sine = row_cos * col_sin + row_sin * col_cos
+    bank[0, :, :HALF] = (real * cosine - imag * sine).astype(BF16)
+    bank[0, :, HALF:] = (real * sine + imag * cosine).astype(BF16)
 
 
 PIECES = 16
@@ -148,12 +149,14 @@
 
 
 def filter_kernel(
-    start_ref, width_ref, shift_ref, target_ref, edge_ref, bank_ref, strain_ref, psd_hbm, row_hbm, twist_hbm, col_hbm,
-    coherent_ref, full_ref, next_ref, after_ref,
-    held, dest, rows, ids, arrived, arrived_ids, chosen, total, bank, relay,
-    turned, crossed, spec, mine, psd_low, psd_high, row, twist, col,
+    start_ref, width_ref, shift_ref, target_ref, edge_ref, bank_ref, strain_ref, psd_hbm,
+    row_hbm, twist_hbm, col_hbm, back_hbm, untwist_hbm, last_hbm,
+    out_hbm,
+    held, dest, rows, ids, arrived, arrived_ids, chosen, total, raw, bank, relay,
+    turned, crossed, spec, coherent, psd_low, psd_high, row, twist, col,
+    back, untwist, last, products, partials, outs,
     row_send, row_recv, id_send, id_recv, bank_send, bank_recv, turn_send, turn_recv,
-    coh_send, coh_recv, pass_send, pass_recv, piece_send, relay_recv, psd_send, psd_recv, table_sem, own_sem,
+    coh_send, coh_recv, out_sem, pass_send, pass_recv, piece_send, relay_recv, psd_send, psd_recv, table_sem, own_sem,
 ):
     me = lax.axis_index("seg")
     det = lax.axis_index("det")
@@ -177,23 +180,25 @@
     fetches = [
         pltpu.make_async_copy(source, held_at, table_sem.at[i])
         for i, (source, held_at) in enumerate(
-            ((row_hbm, row), (twist_hbm.at[det], twist), (col_hbm, col))
+            (
+                (row_hbm, row),
+                (twist_hbm.at[det], twist),
+                (col_hbm, col),
+                (back_hbm, back),
+                (untwist_hbm, untwist),
+                (last_hbm, last),
+            )
         )
     ]
-    for fetch in fetches:
-        fetch.start()
-    shift_bank(det, shift_ref, bank_ref, bank)
-    own_bank = pltpu.make_async_copy(
-        bank.at[det], full_ref.at[pl.ds(det * QV, QV)], own_sem.at[0]
-    )
+    own_bank = pltpu.make_async_copy(bank_ref.at[det], raw.at[det], own_sem.at[0])
     own_bank.start()
     pl.semaphore_wait(barrier, SEGS + DETS - 1)
 
     def bank_copy(o):
         other = (det + o) % DETS
         return pltpu.make_async_remote_copy(
-            src_ref=bank.at[other],
-            dst_ref=full_ref.at[pl.ds(det * QV, QV)],
+            src_ref=bank_ref.at[other],
+            dst_ref=raw.at[det],
             send_sem=bank_send.at[o],
             recv_sem=bank_recv.at[o],
             device_id={"det": other},
@@ -259,6 +264,8 @@
             device_id_type=MESH,
         )
 
+    for fetch in fetches:
+        fetch.start()
     held[...] = strain_ref[...].astype(BF16)
     sort_ranks(me, target_ref, dest, ids)
     step = GROUP * CAP
@@ -287,6 +294,7 @@
     own_bank.wait()
     for o in range(1, DETS):
         bank_copy(o).wait_recv()
+    shift_bank(shift_ref[det], raw, bank)
 
     def whole_pass(source, target, lane, back):
         return pltpu.make_async_remote_copy(
@@ -300,11 +308,11 @@
 
     hot = (me % 32) < 2
     odd = core == 1
-    to_next = whole_pass(full_ref, next_ref, 0, 1)
-    to_after = whole_pass(full_ref, after_ref, 1, 2)
+    to_next = whole_pass(bank.at[0], bank.at[1], 0, 1)
+    to_after = whole_pass(bank.at[0], bank.at[2], 1, 2)
     onward = pltpu.make_async_remote_copy(
-        src_ref=next_ref,
-        dst_ref=after_ref,
+        src_ref=bank.at[1],
+        dst_ref=bank.at[2],
         send_sem=pass_send.at[2],
         recv_sem=pass_recv.at[1],
         device_id={"seg": (me + SEGS - 1) % SEGS},
@@ -315,7 +323,7 @@
 
     def piece_copy(i):
         return pltpu.make_async_remote_copy(
-            src_ref=full_ref.at[pl.ds(i * PIECE, PIECE)],
+            src_ref=bank.at[0, pl.ds(i * PIECE, PIECE)],
             dst_ref=relay,
             send_sem=piece_send.at[i],
             recv_sem=relay_recv.at[0],
@@ -323,10 +331,10 @@
             device_id_type=MESH,
         )
 
-    def last_hop(source, target, lane, at):
+    def last_hop(source, lane, at):
         return pltpu.make_async_remote_copy(
             src_ref=source,
-            dst_ref=target.at[pl.ds(at * PIECE, PIECE)],
+            dst_ref=bank.at[1 + lane, pl.ds(at * PIECE, PIECE)],
             send_sem=piece_send.at[0],
             recv_sem=pass_recv.at[lane],
             device_id={"seg": far},
@@ -355,11 +363,11 @@
 
     @pl.when(jnp.logical_and(hot, odd))
     def _():
-        last_hop(full_ref.at[pl.ds(0, PIECE)], after_ref, 1, 0).start()
+        last_hop(bank.at[0, pl.ds(0, PIECE)], 1, 0).start()
 
     @pl.when(jnp.logical_and(hot, jnp.logical_not(odd)))
     def _():
-        last_hop(full_ref.at[pl.ds(0, PIECE)], next_ref, 0, 0).start()
+        last_hop(bank.at[0, pl.ds(0, PIECE)], 0, 0).start()
 
     own_rows.wait()
     own_ids.wait()
@@ -399,7 +407,7 @@
 
     sample = lax.broadcasted_iota(jnp.int32, (V, QU), 0) * U
     sample = sample + lax.broadcasted_iota(jnp.int32, (V, QU), 1) + det * QU
-    for fetch in fetches:
+    for fetch in fetches[:3]:
         fetch.wait()
     for d in range(DETECTORS):
         begin = start_ref[0, d]
@@ -424,11 +432,11 @@
 
     @pl.when(jnp.logical_and(jnp.logical_not(hot), odd))
     def _():
-        last_hop(relay, after_ref, 1, place).start()
+        last_hop(relay, 1, place).start()
 
     @pl.when(jnp.logical_and(jnp.logical_not(hot), jnp.logical_not(odd)))
     def _():
-        last_hop(relay, next_ref, 0, place).start()
+        last_hop(relay, 0, place).start()
 
     high = DETECTORS * SHARE
     row_at = lax.broadcasted_iota(jnp.int32, (high, high), 0)
@@ -478,31 +486,84 @@
             rows_of = slice(d * SHARE, (d + 1) * SHARE)
             direct = direct + psd_low[d] * spec[0, rows_of, cols]
             mirrored = mirrored + psd_high[d, 1 : SHARE + 1] * spec[1, rows_of, cols]
-        mine[:SHARE, cols] = direct.astype(BF16)
-        mine[SHARE:, cols] = mirrored.astype(BF16)
-
-    def coherent_copy(o):
-        return pltpu.make_async_remote_copy(
-            src_ref=mine,
-            dst_ref=coherent_ref.at[pl.ds(det * QV, QV)],
-            send_sem=coh_send.at[o],
-            recv_sem=coh_recv.at[o],
-            device_id={"det": (det + o) % DETS},
-            device_id_type=MESH,
-        )
-
-    for o in (2, 1, 3):
-        coherent_copy(o).start()
-    keep = pltpu.make_async_copy(mine, coherent_ref.at[pl.ds(det * QV, QV)], own_sem.at[3])
-    keep.start()
-
+        coherent[det, :SHARE, cols] = direct.astype(BF16)
+        coherent[det, SHARE:, cols] = mirrored.astype(BF16)
+
+    near = det + 1 - 2 * (det % 2)
+    entry = DETS // 2 - det // 2
+    beyond = DETS - 1 - det // 2 * (DETS - 1)
+    middle = jnp.logical_or(det == 1, det == 2)
+
+    def coherent_copy(block, other, lane):
+        return pltpu.make_async_remote_copy(
+            src_ref=coherent.at[block],
+            dst_ref=coherent.at[block],
+            send_sem=coh_send.at[lane],
+            recv_sem=coh_recv.at[block],
+            device_id={"det": other},
+            device_id_type=MESH,
+        )
+
+    coherent_copy(det, entry, 0).start()
+    coherent_copy(det, near, 1).start()
     to_next.wait_recv()
 
     @pl.when(odd)
     def _():
         onward.start()
 
+    for fetch in fetches[3:]:
+        fetch.wait()
+
+    def multiply(block, r):
+        real = coherent[block, :, :HALF].astype(F32)
+        imag = coherent[block, :, HALF:].astype(F32)
+        at = pl.ds(pl.multiple_of(block * QV, QV), QV)
+        other_real = bank[r, at, :HALF].astype(F32)
+        other_imag = bank[r, at, HALF:].astype(F32)
+        into = slice(r * QV, (r + 1) * QV)
+        products[into, :HALF] = (real * other_real + imag * other_imag).astype(BF16)
+        products[into, HALF:] = (imag * other_real - real * other_imag).astype(BF16)
+
+    def invert(block):
+        for r in range(STEPS):
+            multiply(block, r)
+        for half in range(2):
+            lanes = slice(half * HALF, (half + 1) * HALF)
+            upper = slice(U + half * HALF, U + (half + 1) * HALF)
+            first = jnp.dot(products[...], back[:, lanes], preferred_element_type=F32)
+            second = jnp.dot(products[...], back[:, upper], preferred_element_type=F32)
+            cosine, sine = untwist[block, 0, :, lanes], untwist[block, 1, :, lanes]
+            for r in range(STEPS):
+                real, imag = first[r * QV : (r + 1) * QV], second[r * QV : (r + 1) * QV]
+                partials[r, 0, block, :, lanes] = (real * cosine - imag * sine).astype(BF16)
+                partials[r, 1, block, :, lanes] = (real * sine + imag * cosine).astype(BF16)
+
     to_after.wait_recv()
+    invert(det)
+    coherent_copy(near, det, 1).wait_recv()
+    invert(near)
+    coherent_copy(entry, det, 0).wait_recv()
+
+    @pl.when(middle)
+    def _():
+        coherent_copy(entry, near, 2).start()
+        coherent_copy(beyond, det, 0).wait_recv()
+        coherent_copy(beyond, near, 3).start()
+
+    invert(entry)
+
+    @pl.when(jnp.logical_not(middle))
+    def _():
+        coherent_copy(beyond, det, 0).wait_recv()
+
+    invert(beyond)
+    outgoing = []
+    for r in range(STEPS):
+        made = jnp.dot(last[...], partials[r].reshape(2 * V, U), preferred_element_type=F32)
+        outs[r] = made.astype(BF16).reshape(V // 2, 2, U)
+        outgoing.append(pltpu.make_async_copy(outs.at[r], out_hbm.at[0, 0, r], out_sem.at[r]))
+        outgoing[r].start()
 
     @pl.when(upper_det)
     def _():
@@ -513,7 +574,6 @@
     def _():
         to_low.wait_send()
 
-
     @pl.when(jnp.logical_or(odd, jnp.logical_not(hot)))
     def _():
         to_next.wait_send()
@@ -526,7 +586,7 @@
     def _():
         lax.fori_loop(1, PIECES, pieces_sent, 0)
 
-    last_hop(relay, next_ref, 0, place).wait_send()
+    last_hop(relay, 0, place).wait_send()
 
     @pl.when(odd)
     def _():
@@ -542,19 +602,25 @@
         bank_copy(o).wait_send()
         for d in range(DETECTORS):
             turn_copy(o, d).wait_send()
-    for o in (1, 3, 2):
-        coherent_copy(o).wait()
-    keep.wait()
-
-
-def filtered(start, width, shift, target, edge, bank, strain, psd, row, twist, col):
-    whole = jax.ShapeDtypeStruct((V, U), BF16)
+    coherent_copy(det, entry, 0).wait_send()
+    coherent_copy(det, near, 1).wait_send()
+
+    @pl.when(middle)
+    def _():
+        coherent_copy(entry, near, 2).wait_send()
+        coherent_copy(beyond, near, 3).wait_send()
+
+    for leaving in outgoing:
+        leaving.wait()
+
+
+def filtered(*operands):
     dma = pltpu.SemaphoreType.DMA
     return pl.pallas_call(
         filter_kernel,
-        out_shape=(whole,) * 4,
-        in_specs=[SM, SM, SM, VM, VM, VM, VM, HB, HB, HB, HB],
-        out_specs=(HB,) * 4,
+        out_shape=jax.ShapeDtypeStruct((1, 1, STEPS, V // 2, 2, U), BF16),
+        in_specs=[SM, SM, SM, VM, VM, HB, VM] + [HB] * 7,
+        out_specs=HB,
         scratch_shapes=[
             pltpu.VMEM((SLOTS, QU), BF16),
             pltpu.VMEM((16, LANES), jnp.int32),
@@ -564,22 +630,29 @@
             pltpu.VMEM((SEGS, 1, 128), jnp.int32),
             pltpu.VMEM((ROWS, GROUP * 64), BF16),
             pltpu.VMEM((ROWS, QU), F32),
-            pltpu.VMEM((BLOCK, QV, U), BF16),
+            pltpu.VMEM((DETS, QV, 2, HALF), BF16),
+            pltpu.VMEM((STEPS, V, U), BF16),
             pltpu.VMEM((PIECE, U), BF16),
             pltpu.VMEM((DETS, DETECTORS, SHARE, 2 * QU), BF16),
             pltpu.VMEM((DETS, DETECTORS, SHARE, 2 * QU), BF16),
             pltpu.VMEM((2, DETECTORS * SHARE, U), F32),
-            pltpu.VMEM((QV, U), BF16),
+            pltpu.VMEM((DETS, QV, U), BF16),
             pltpu.VMEM((DETECTORS, SHARE, HALF), F32),
             pltpu.VMEM((DETECTORS, SHARE + 8, HALF), F32),
             pltpu.VMEM((V, V), BF16),
             pltpu.VMEM((2, V // 2, QU), F32),
             pltpu.VMEM((2, DETS, 2 * QU, U), BF16),
+            pltpu.VMEM((U, 2 * U), BF16),
+            pltpu.VMEM((DETS, 2, QV, U), F32),
+            pltpu.VMEM((V, 2 * V), BF16),
+            pltpu.VMEM((STEPS * QV, U), BF16),
+            pltpu.VMEM((STEPS, 2, DETS, QV, U), BF16),
+            pltpu.VMEM((STEPS, V // 2, 2, U), BF16),
             dma((SEGS,)), dma((SEGS,)), dma((SEGS,)), dma((SEGS,)),
             dma((DETS,)), dma((DETS,)),
             dma((DETS, DETECTORS)), dma((DETS, DETECTORS)),
-            dma((DETS,)), dma((DETS,)),
-            dma((3,)), dma((2,)), dma((PIECES,)), dma((1,)), dma((2,)), dma((2,)), dma((3,)), dma((5,)),
+            dma((4,)), dma((DETS,)), dma((STEPS,)),
+            dma((3,)), dma((2,)), dma((PIECES,)), dma((1,)), dma((2,)), dma((2,)), dma((6,)), dma((5,)),
         ],
         compiler_params=pltpu.CompilerParams(
             vmem_limit_bytes=LIMIT, collective_id=0, has_side_effects=True
@@ -588,91 +661,12 @@
             flops=12_000_000_000, bytes_accessed=16_000_000, transcendentals=0
         ),
         name="filtered",
-    )(start, width, shift, target, edge, bank, strain, psd, row, twist, col)
-
-
-CHUNK = 256
-
-
-def inverse_kernel(
-    coherent_hbm, first_hbm, second_hbm, third_hbm, perm_hbm, back_hbm, untwist_hbm, last_hbm, out_hbm,
-    coherent, banks, perm, back, untwist, last, products, partials, outs, load_sem, out_sem,
-):
-    loads = [
-        pltpu.make_async_copy(source, target, load_sem.at[i])
-        for i, (source, target) in enumerate(
-            (
-                (coherent_hbm, coherent),
-                (perm_hbm, perm),
-                (first_hbm, banks.at[0]),
-                (back_hbm, back),
-                (untwist_hbm, untwist),
-                (last_hbm, last),
-                (second_hbm, banks.at[1]),
-                (third_hbm, banks.at[2]),
-            )
-        )
-    ]
-    for load in loads:
-        load.start()
-    loads[0].wait()
-    loads[1].wait()
-    whole = jnp.dot(perm[...], coherent[...], preferred_element_type=F32).astype(BF16)
-    coherent[...] = whole
-    outgoing = []
-    for r in range(STEPS):
-        loads[(2, 6, 7)[r]].wait()
-        real, imag = coherent[:, :HALF].astype(F32), coherent[:, HALF:].astype(F32)
-        other_real = banks[r, :, :HALF].astype(F32)
-        other_imag = banks[r, :, HALF:].astype(F32)
-        products[r, :, :HALF] = (real * other_real + imag * other_imag).astype(BF16)
-        products[r, :, HALF:] = (imag * other_real - real * other_imag).astype(BF16)
-        if r == 0:
-            for i in (3, 4, 5):
-                loads[i].wait()
-        for c in range(U // CHUNK):
-            lanes = slice(c * CHUNK, (c + 1) * CHUNK)
-            upper = slice(U + c * CHUNK, U + (c + 1) * CHUNK)
-            first = jnp.dot(products[r], back[:, lanes], preferred_element_type=F32)
-            second = jnp.dot(products[r], back[:, upper], preferred_element_type=F32)
-            cosine, sine = untwist[0, :, lanes], untwist[1, :, lanes]
-            partials[c % 2, :V] = (first * cosine - second * sine).astype(BF16)
-            partials[c % 2, V:] = (first * sine + second * cosine).astype(BF16)
-            made = jnp.dot(last[...], partials[c % 2], preferred_element_type=F32).astype(BF16)
-            outs[r, :, :, lanes] = made.reshape(V // 2, 2, CHUNK)
-        outgoing.append(pltpu.make_async_copy(outs.at[r], out_hbm.at[0, 0, r], out_sem.at[r]))
-        outgoing[r].start()
-    for leaving in outgoing:
-        leaving.wait()
-
-
-def inverse_steps(coherent, banks, perm, back, untwist, last):
-    return pl.pallas_call(
-        inverse_kernel,
-        out_shape=jax.ShapeDtypeStruct((1, 1, STEPS, V // 2, 2, U), BF16),
-        in_specs=[HB] * 8,
-        out_specs=HB,
-        scratch_shapes=[
-            pltpu.VMEM((V, U), BF16),
-            pltpu.VMEM((STEPS, V, U), BF16),
-            pltpu.VMEM((V, V), BF16),
-            pltpu.VMEM((U, 2 * U), BF16),
-            pltpu.VMEM((2, V, U), F32),
-            pltpu.VMEM((V, 2 * V), BF16),
-            pltpu.VMEM((STEPS, V, U), BF16),
-            pltpu.VMEM((2, 2 * V, CHUNK), BF16),
-            pltpu.VMEM((STEPS, V // 2, 2, U), BF16),
-            pltpu.SemaphoreType.DMA((8,)),
-            pltpu.SemaphoreType.DMA((STEPS,)),
-        ],
-        compiler_params=pltpu.CompilerParams(vmem_limit_bytes=LIMIT),
-        name="inverse_steps",
-    )(coherent, *banks, perm, back, untwist, last)
+    )(*operands)
 
 
 def body(strain, row_target, gate_start, gate_width, inverse_psd, templates, template_shift):
-    row, twist, edge, col, perm, back, untwist, last = (jnp.asarray(t) for t in tables())
-    coherent, *banks = filtered(
+    row, twist, edge, col, back, untwist, last = (jnp.asarray(t) for t in tables())
+    return filtered(
         gate_start,
         gate_width,
         template_shift,
@@ -684,8 +678,10 @@
         row,
         twist,
         col,
+        back,
+        untwist,
+        last,
     )
-    return inverse_steps(coherent, banks, perm, back, untwist, last)
 
 
 def solution(mesh):

time: 164 us -> 153 us (0.933)
  the two profiles are of different devices: /device:TPU:95 before, /device:TPU:14 now
where the time goes in v4:
time: 153 us; the launch traced here: 152 us
  Pallas kernels  147 us (96%)
  local copies, waits for them, and re-layouts  5.71 us (4%)
    pallas_call x1, Pallas kernels, filtered(): pl.pallas_call(filter_kernel, out_shape=jax.ShapeDtypeStruct((1, 1, STEPS...  147 us
    unnamed x1, local copies, waits for them, and re-layouts  5.71 us

profile of v4, /device:TPU:14, one launch (start us, length us, event | category | flops | bytes accessed | tf_op | source)
XLA Modules:
  0.0 152.4 jit_solution(17121644569290440837)
XLA Ops:
  0.0 146.7 %filtered.1 = bf16[1,1,3,256,2,1024]{5,4,3,2,1,0:T(2,128)(2,1)} custom-call(s32[1,3]{1,0:T(1,128)} %start_ref.1, s32[1,3]{1,0:T(1,128)} %width_ref.1, s32[4]{0:T(128)} %shift_ref.1, s32[3072]{0:T(1024)} %target_ref.1, f32[4,8,512]{2,1,0:T(8,128)} %constant.16.clone.edge_ref, bf16[4,128,2,512]{3,2,1,0:T(2,128)(2,1)} %bank_ref.1, f32[3072,256]{1,0:T(8,128)} %strain_ref.1, ...), custom_call_target="tpu_custom_call" | custom-call | flops 12000000000 | bytes 16000000 | tf_op jit(solution)/shard_map/filtered/pallas_call | solution.py:619
  146.7 5.7 %copy.16 = bf16[1,1,3,256,2,1024]{5,4,3,2,1,0:T(2,128)(2,1)} copy(bf16[1,1,3,256,2,1024]{5,4,3,2,1,0:T(2,128)(2,1)} %filtered.1) | data formatting | bytes 6291456

commit v5 on v4

--- a/solution.py
+++ b/solution.py
@@ -83,6 +83,7 @@
 
 
 GROUP = 16
+BATCH = 8
 LANES = 256
 COUNT = SLOTS // LANES
 
@@ -145,16 +146,18 @@
 
 
 PIECES = 16
+PART = 32
+PARTS = QV // PART
 PIECE = V // PIECES
 
 
 def filter_kernel(
-    start_ref, width_ref, shift_ref, target_ref, edge_ref, bank_ref, strain_ref, psd_hbm,
-    row_hbm, twist_hbm, col_hbm, back_hbm, untwist_hbm, last_hbm,
+    start_ref, width_ref, shift_ref, target_ref, edge_ref, bank_ref, strain_hbm, psd_hbm,
+    row_hbm, twist_hbm, col_hbm, back_hbm, untwist_hbm,
     out_hbm,
-    held, dest, rows, ids, arrived, arrived_ids, chosen, total, raw, bank, relay,
+    strain, held, dest, rows, ids, arrived, arrived_ids, chosen, total, raw, bank, relay,
     turned, crossed, spec, coherent, psd_low, psd_high, row, twist, col,
-    back, untwist, last, products, partials, outs,
+    back, untwist, products, partials,
     row_send, row_recv, id_send, id_recv, bank_send, bank_recv, turn_send, turn_recv,
     coh_send, coh_recv, out_sem, pass_send, pass_recv, piece_send, relay_recv, psd_send, psd_recv, table_sem, own_sem,
 ):
@@ -163,6 +166,8 @@
     core = me % 2
     place = (me % 32) // 2
     barrier = pltpu.get_barrier_semaphore()
+    own_strain = pltpu.make_async_copy(strain_hbm, strain, own_sem.at[3])
+    own_strain.start()
 
     def greet(o, _):
         pl.semaphore_signal(
@@ -186,7 +191,6 @@
                 (col_hbm, col),
                 (back_hbm, back),
                 (untwist_hbm, untwist),
-                (last_hbm, last),
             )
         )
     ]
@@ -266,7 +270,8 @@
 
     for fetch in fetches:
         fetch.start()
-    held[...] = strain_ref[...].astype(BF16)
+    own_strain.wait()
+    held[...] = strain[...].astype(BF16)
     sort_ranks(me, target_ref, dest, ids)
     step = GROUP * CAP
 
@@ -377,17 +382,17 @@
         row_copy(o).wait_recv()
         return 0
 
-    wide = GROUP * 64
-    groups = SEGS // GROUP
+    wide = BATCH * 64
+    groups = SEGS // BATCH
     for g in range(groups):
-        lax.fori_loop(max(1, g * GROUP), (g + 1) * GROUP, receive, 0)
-        for p in range(GROUP // 2):
-            o = g * GROUP + 2 * p
+        lax.fori_loop(max(1, g * BATCH), (g + 1) * BATCH, receive, 0)
+        for p in range(BATCH // 2):
+            o = g * BATCH + 2 * p
             ident = arrived_ids[o] + arrived_ids[o + 1] - 1
             chosen[:, p * 128 : (p + 1) * 128] = jnp.where(
                 lax.broadcasted_iota(jnp.int32, (ROWS, 128), 0) == ident, 1.0, 0.0
             ).astype(BF16)
-        block = arrived[g * GROUP : (g + 1) * GROUP].reshape(wide, QU)
+        block = arrived[g * BATCH : (g + 1) * BATCH].reshape(wide, QU)
         part = jnp.dot(chosen[...], block, preferred_element_type=F32)
         if g == 0:
             total[...] = part
@@ -437,6 +442,34 @@
     @pl.when(jnp.logical_and(jnp.logical_not(hot), jnp.logical_not(odd)))
     def _():
         last_hop(relay, 0, place).start()
+
+    near = det + 1 - 2 * (det % 2)
+    entry = DETS // 2 - det // 2
+    beyond = DETS - 1 - det // 2 * (DETS - 1)
+    middle = jnp.logical_or(det == 1, det == 2)
+
+    def coherent_copy(block, other, lane, part):
+        rows_of = pl.ds(part * PART, PART)
+        return pltpu.make_async_remote_copy(
+            src_ref=coherent.at[block, rows_of],
+            dst_ref=coherent.at[block, rows_of],
+            send_sem=coh_send.at[lane, part],
+            recv_sem=coh_recv.at[block, part],
+            device_id={"det": other},
+            device_id_type=MESH,
+        )
+
+    def gather_rows(which, scale, shift, first_row):
+        for half in range(2):
+            cols = slice(half * HALF, (half + 1) * HALF)
+            value = 0.0
+            for d in range(DETECTORS):
+                held_rows = spec[which, d * SHARE : (d + 1) * SHARE, cols]
+                value = value + scale[d, shift : shift + SHARE] * held_rows
+            coherent[det, first_row : first_row + SHARE, cols] = value.astype(BF16)
+        for part in range(first_row // PART, (first_row + SHARE) // PART):
+            coherent_copy(det, entry, 0, part).start()
+            coherent_copy(det, near, 1, part).start()
 
     high = DETECTORS * SHARE
     row_at = lax.broadcasted_iota(jnp.int32, (high, high), 0)
@@ -460,52 +493,32 @@
         twin = jnp.concatenate([twin, twin], axis=1) * edge_ref[source][:1]
         mirrored = jnp.where(packed, twin, wide_came).astype(BF16)
         mirrored = jnp.dot(flip, mirrored, preferred_element_type=F32).astype(BF16)
+        if o == 2:
+
+            @pl.when(upper_det)
+            def _():
+                to_low.wait_recv()
+                keep_high.wait()
+
+            @pl.when(jnp.logical_not(upper_det))
+            def _():
+                to_high.wait_recv()
+                to_rest.wait_recv()
+                keep_low.wait()
+
         part = jnp.dot(direct, col[0, source], preferred_element_type=F32)
+        if o == 0:
+            spec[0] = part
+        else:
+            spec[0] += part
+        if o == 2:
+            gather_rows(0, psd_low, 0, 0)
         other = jnp.dot(mirrored, col[1, source], preferred_element_type=F32)
         if o == 0:
-            spec[0], spec[1] = part, other
+            spec[1] = other
         else:
-            spec[0] += part
             spec[1] += other
-
-    @pl.when(upper_det)
-    def _():
-        to_low.wait_recv()
-        keep_high.wait()
-
-    @pl.when(jnp.logical_not(upper_det))
-    def _():
-        to_high.wait_recv()
-        to_rest.wait_recv()
-        keep_low.wait()
-
-    for half in range(2):
-        cols = slice(half * HALF, (half + 1) * HALF)
-        direct, mirrored = 0.0, 0.0
-        for d in range(DETECTORS):
-            rows_of = slice(d * SHARE, (d + 1) * SHARE)
-            direct = direct + psd_low[d] * spec[0, rows_of, cols]
-            mirrored = mirrored + psd_high[d, 1 : SHARE + 1] * spec[1, rows_of, cols]
-        coherent[det, :SHARE, cols] = direct.astype(BF16)
-        coherent[det, SHARE:, cols] = mirrored.astype(BF16)
-
-    near = det + 1 - 2 * (det % 2)
-    entry = DETS // 2 - det // 2
-    beyond = DETS - 1 - det // 2 * (DETS - 1)
-    middle = jnp.logical_or(det == 1, det == 2)
-
-    def coherent_copy(block, other, lane):
-        return pltpu.make_async_remote_copy(
-            src_ref=coherent.at[block],
-            dst_ref=coherent.at[block],
-            send_sem=coh_send.at[lane],
-            recv_sem=coh_recv.at[block],
-            device_id={"det": other},
-            device_id_type=MESH,
-        )
-
-    coherent_copy(det, entry, 0).start()
-    coherent_copy(det, near, 1).start()
+    gather_rows(1, psd_high, 1, SHARE)
     to_next.wait_recv()
 
     @pl.when(odd)
@@ -524,6 +537,11 @@
         into = slice(r * QV, (r + 1) * QV)
         products[into, :HALF] = (real * other_real + imag * other_imag).astype(BF16)
         products[into, HALF:] = (imag * other_real - real * other_imag).astype(BF16)
+
+    def leave(block):
+        return pltpu.make_async_copy(
+            partials.at[:, :, block], out_hbm.at[:, :, block], out_sem.at[block]
+        )
 
     def invert(block):
         for r in range(STEPS):
@@ -538,32 +556,37 @@
                 real, imag = first[r * QV : (r + 1) * QV], second[r * QV : (r + 1) * QV]
                 partials[r, 0, block, :, lanes] = (real * cosine - imag * sine).astype(BF16)
                 partials[r, 1, block, :, lanes] = (real * sine + imag * cosine).astype(BF16)
+        leave(block).start()
+
+    def arrive(block):
+        for part in range(PARTS):
+            coherent_copy(block, det, 0, part).wait_recv()
 
     to_after.wait_recv()
     invert(det)
-    coherent_copy(near, det, 1).wait_recv()
+
+    @pl.when(middle)
+    def _():
+        for part in range(PARTS):
+            coherent_copy(entry, det, 0, part).wait_recv()
+            coherent_copy(entry, near, 2, part).start()
+            coherent_copy(beyond, det, 0, part).wait_recv()
+            coherent_copy(beyond, near, 3, part).start()
+
+    arrive(near)
     invert(near)
-    coherent_copy(entry, det, 0).wait_recv()
-
-    @pl.when(middle)
-    def _():
-        coherent_copy(entry, near, 2).start()
-        coherent_copy(beyond, det, 0).wait_recv()
-        coherent_copy(beyond, near, 3).start()
+
+    @pl.when(jnp.logical_not(middle))
+    def _():
+        arrive(entry)
 
     invert(entry)
 
     @pl.when(jnp.logical_not(middle))
     def _():
-        coherent_copy(beyond, det, 0).wait_recv()
+        arrive(beyond)
 
     invert(beyond)
-    outgoing = []
-    for r in range(STEPS):
-        made = jnp.dot(last[...], partials[r].reshape(2 * V, U), preferred_element_type=F32)
-        outs[r] = made.astype(BF16).reshape(V // 2, 2, U)
-        outgoing.append(pltpu.make_async_copy(outs.at[r], out_hbm.at[0, 0, r], out_sem.at[r]))
-        outgoing[r].start()
 
     @pl.when(upper_det)
     def _():
@@ -602,33 +625,36 @@
         bank_copy(o).wait_send()
         for d in range(DETECTORS):
             turn_copy(o, d).wait_send()
-    coherent_copy(det, entry, 0).wait_send()
-    coherent_copy(det, near, 1).wait_send()
+    for part in range(PARTS):
+        coherent_copy(det, entry, 0, part).wait_send()
+        coherent_copy(det, near, 1, part).wait_send()
 
     @pl.when(middle)
     def _():
-        coherent_copy(entry, near, 2).wait_send()
-        coherent_copy(beyond, near, 3).wait_send()
-
-    for leaving in outgoing:
-        leaving.wait()
+        for part in range(PARTS):
+            coherent_copy(entry, near, 2, part).wait_send()
+            coherent_copy(beyond, near, 3, part).wait_send()
+
+    for block in range(DETS):
+        leave(block).wait()
 
 
 def filtered(*operands):
     dma = pltpu.SemaphoreType.DMA
     return pl.pallas_call(
         filter_kernel,
-        out_shape=jax.ShapeDtypeStruct((1, 1, STEPS, V // 2, 2, U), BF16),
-        in_specs=[SM, SM, SM, VM, VM, HB, VM] + [HB] * 7,
+        out_shape=jax.ShapeDtypeStruct((STEPS, 2, DETS, QV, U), BF16),
+        in_specs=[SM, SM, SM, VM, VM] + [HB] * 8,
         out_specs=HB,
         scratch_shapes=[
+            pltpu.VMEM((SLOTS, QU), F32),
             pltpu.VMEM((SLOTS, QU), BF16),
             pltpu.VMEM((16, LANES), jnp.int32),
             pltpu.VMEM((SLOTS, QU), BF16),
             pltpu.VMEM((SEGS, 1, 128), jnp.int32),
             pltpu.VMEM((SEGS, 64, QU), BF16),
             pltpu.VMEM((SEGS, 1, 128), jnp.int32),
-            pltpu.VMEM((ROWS, GROUP * 64), BF16),
+            pltpu.VMEM((ROWS, BATCH * 64), BF16),
             pltpu.VMEM((ROWS, QU), F32),
             pltpu.VMEM((DETS, QV, 2, HALF), BF16),
             pltpu.VMEM((STEPS, V, U), BF16),
@@ -644,15 +670,13 @@
             pltpu.VMEM((2, DETS, 2 * QU, U), BF16),
             pltpu.VMEM((U, 2 * U), BF16),
             pltpu.VMEM((DETS, 2, QV, U), F32),
-            pltpu.VMEM((V, 2 * V), BF16),
             pltpu.VMEM((STEPS * QV, U), BF16),
             pltpu.VMEM((STEPS, 2, DETS, QV, U), BF16),
-            pltpu.VMEM((STEPS, V // 2, 2, U), BF16),
             dma((SEGS,)), dma((SEGS,)), dma((SEGS,)), dma((SEGS,)),
             dma((DETS,)), dma((DETS,)),
             dma((DETS, DETECTORS)), dma((DETS, DETECTORS)),
-            dma((4,)), dma((DETS,)), dma((STEPS,)),
-            dma((3,)), dma((2,)), dma((PIECES,)), dma((1,)), dma((2,)), dma((2,)), dma((6,)), dma((5,)),
+            dma((4, PARTS)), dma((DETS, PARTS)), dma((DETS,)),
+            dma((3,)), dma((2,)), dma((PIECES,)), dma((1,)), dma((2,)), dma((2,)), dma((5,)), dma((5,)),
         ],
         compiler_params=pltpu.CompilerParams(
             vmem_limit_bytes=LIMIT, collective_id=0, has_side_effects=True
@@ -664,9 +688,32 @@
     )(*operands)
 
 
+COLUMNS = 512
+
+
+def last_kernel(partial_ref, last_ref, out_ref):
+    made = jnp.dot(last_ref[...], partial_ref[0], preferred_element_type=F32)
+    out_ref[0, 0, 0] = made.astype(BF16).reshape(V // 2, 2, COLUMNS)
+
+
+def last_rows(partials, last):
+    return pl.pallas_call(
+        last_kernel,
+        grid=(STEPS, U // COLUMNS),
+        out_shape=jax.ShapeDtypeStruct((1, 1, STEPS, V // 2, 2, U), BF16),
+        in_specs=[
+            pl.BlockSpec((1, 2 * V, COLUMNS), lambda r, c: (r, 0, c)),
+            pl.BlockSpec((V, 2 * V), lambda r, c: (0, 0)),
+        ],
+        out_specs=pl.BlockSpec((1, 1, 1, V // 2, 2, COLUMNS), lambda r, c: (0, 0, r, 0, 0, c)),
+        compiler_params=pltpu.CompilerParams(vmem_limit_bytes=LIMIT),
+        name="last_rows",
+    )(partials, last)
+
+
 def body(strain, row_target, gate_start, gate_width, inverse_psd, templates, template_shift):
     row, twist, edge, col, back, untwist, last = (jnp.asarray(t) for t in tables())
-    return filtered(
+    partials = filtered(
         gate_start,
         gate_width,
         template_shift,
@@ -680,8 +727,8 @@
         col,
         back,
         untwist,
-        last,
     )
+    return last_rows(partials.reshape(STEPS, 2 * V, U), last)
 
 
 def solution(mesh):

time: 153 us -> 143 us (0.935)
  local copies, waits for them, and re-layouts: 5.71 us -> 0 us
  Pallas kernels: 147 us -> 143 us
    unnamed x1 -> x0, local copies, waits for them, and re-layouts: 5.71 us -> none
    pallas_call x1 -> x2, Pallas kernels: 147 us -> 143 us  [the longest x1 135 us: filtered(): pl.pallas_call(filter_kernel, out_shape=jax.ShapeDtypeStruct((STEPS, 2, D...]
where the time goes in v5:
time: 143 us
  Pallas kernels  143 us (100%)
    pallas_call x1, Pallas kernels, filtered(): pl.pallas_call(filter_kernel, out_shape=jax.ShapeDtypeStruct((STEPS, 2, D...  135 us
    pallas_call x1, Pallas kernels, last_rows(): pl.pallas_call(last_kernel, grid=(STEPS, U // COLUMNS), out_shape=jax.Sha...  8.26 us

profile of v5, /device:TPU:14, one launch (start us, length us, event | category | flops | bytes accessed | tf_op | source)
XLA Modules:
  0.0 143.1 jit_solution(3840523853487425432)
XLA Ops:
  0.0 134.8 %filtered.1 = bf16[3,2,4,128,1024]{4,3,2,1,0:T(8,128)(2,1)} custom-call(s32[1,3]{1,0:T(1,128)} %start_ref.1, s32[1,3]{1,0:T(1,128)} %width_ref.1, s32[4]{0:T(128)} %shift_ref.1, s32[3072]{0:T(1024)} %target_ref.1, f32[4,8,512]{2,1,0:T(8,128)} %constant.16.clone.edge_ref, bf16[4,128,2,512]{3,2,1,0:T(2,128)(2,1)} %bank_ref.1, f32[3072,256]{1,0:T(8,128)} %strain_hbm.1, ...), custom_call_target="tpu_custom_call" | custom-call | flops 12000000000 | bytes 16000000 | tf_op jit(solution)/shard_map/filtered/pallas_call | solution.py:644
  134.8 8.3 %last_rows.1 = bf16[1,1,3,256,2,1024]{5,4,3,2,1,0:T(2,128)(2,1)} custom-call(bf16[3,1024,1024]{2,1,0:T(8,128)(2,1)} %bitcast.1, bf16[512,1024]{1,0:T(8,128)(2,1)} %constant.20.clone.last_ref), custom_call_target="tpu_custom_call" | custom-call | tf_op jit(solution)/shard_map/last_rows/pallas_call | solution.py:700

commit v6 on v5

--- a/solution.py
+++ b/solution.py
@@ -85,6 +85,7 @@
 GROUP = 16
 BATCH = 8
 LANES = 256
+HOME = SEGS // 2
 COUNT = SLOTS // LANES
 
 
@@ -101,7 +102,9 @@
         t = target_ref[b * LANES : (b + 1) * LANES].reshape(1, LANES)
         owner = ((t >> 9) * 43691) >> 17
         local = t - owner * ROWS
-        owner = jnp.where(t >= 0, (owner + SEGS - me) & (SEGS - 1), SEGS)
+        flips = ((owner >> 5) + me // HOME) & 1
+        slot = ((owner + SEGS - me) & (HOME - 1)) + HOME - HOME * flips
+        owner = jnp.where(t >= 0, slot, SEGS)
         mine = jnp.where(seg == owner, 1.0, 0.0)
         before = jnp.dot(mine.astype(BF16), upper, preferred_element_type=F32)
         rank = jnp.sum(mine * (before + carry), axis=0, keepdims=True).astype(jnp.int32) - 1
@@ -248,13 +251,16 @@
         to_low.start()
         keep_low.start()
 
+    def partner(o):
+        return (me // HOME + 1 + o // HOME) % 2 * HOME + (me % HOME + o) % HOME
+
     def row_copy(o):
         return pltpu.make_async_remote_copy(
             src_ref=rows.at[pl.ds(o * CAP, CAP)],
             dst_ref=arrived.at[o, pl.ds(0, CAP)],
             send_sem=row_send.at[o],
             recv_sem=row_recv.at[o],
-            device_id={"seg": (me + o) % SEGS},
+            device_id={"seg": partner(o)},
             device_id_type=MESH,
         )
 
@@ -264,7 +270,7 @@
             dst_ref=arrived_ids.at[o],
             send_sem=id_send.at[o],
             recv_sem=id_recv.at[o],
-            device_id={"seg": (me + o) % SEGS},
+            device_id={"seg": partner(o)},
             device_id_type=MESH,
         )
 
@@ -287,12 +293,12 @@
         ]
         picked = jnp.dot(jnp.concatenate(picks, axis=1), held[...], preferred_element_type=F32)
         rows[g * step : (g + 1) * step] = picked.astype(BF16)
-        lax.fori_loop(max(1, g * GROUP), (g + 1) * GROUP, send, 0)
+        lax.fori_loop(g * GROUP + (g * GROUP == HOME), (g + 1) * GROUP, send, 0)
     own_rows = pltpu.make_async_copy(
-        rows.at[pl.ds(0, CAP)], arrived.at[0, pl.ds(0, CAP)], own_sem.at[1]
+        rows.at[pl.ds(HOME * CAP, CAP)], arrived.at[HOME, pl.ds(0, CAP)], own_sem.at[1]
     )
     own_rows.start()
-    own_ids = pltpu.make_async_copy(ids.at[0], arrived_ids.at[0], own_sem.at[2])
+    own_ids = pltpu.make_async_copy(ids.at[HOME], arrived_ids.at[HOME], own_sem.at[2])
     own_ids.start()
     arrived[:, CAP:, :] = jnp.zeros((SEGS, 64 - CAP, QU), BF16)
 
@@ -384,8 +390,8 @@
 
     wide = BATCH * 64
     groups = SEGS // BATCH
-    for g in range(groups):
-        lax.fori_loop(max(1, g * BATCH), (g + 1) * BATCH, receive, 0)
+    for g in (*range(groups // 2, groups), *range(groups // 2)):
+        lax.fori_loop(g * BATCH + (g * BATCH == HOME), (g + 1) * BATCH, receive, 0)
         for p in range(BATCH // 2):
             o = g * BATCH + 2 * p
             ident = arrived_ids[o] + arrived_ids[o + 1] - 1
@@ -394,7 +400,7 @@
             ).astype(BF16)
         block = arrived[g * BATCH : (g + 1) * BATCH].reshape(wide, QU)
         part = jnp.dot(chosen[...], block, preferred_element_type=F32)
-        if g == 0:
+        if g == groups // 2:
             total[...] = part
         else:
             total[...] += part
@@ -620,7 +626,8 @@
         row_copy(o).wait_send()
         return 0
 
-    lax.fori_loop(1, SEGS, sent, 0)
+    lax.fori_loop(0, HOME, sent, 0)
+    lax.fori_loop(HOME + 1, SEGS, sent, 0)
     for o in range(1, DETS):
         bank_copy(o).wait_send()
         for d in range(DETECTORS):

time: 143 us -> 137 us (0.958); the launches traced: 143 us -> 135 us
  Pallas kernels: 143 us -> 135 us
    pallas_call x1, Pallas kernels: 135 us -> 127 us  [filtered(): pl.pallas_call(filter_kernel, out_shape=jax.ShapeDtypeStruct((STEPS, 2, D...]
where the time goes in v6:
time: 137 us; the launch traced here: 135 us
  Pallas kernels  135 us (99%)
    pallas_call x1, Pallas kernels, filtered(): pl.pallas_call(filter_kernel, out_shape=jax.ShapeDtypeStruct((STEPS, 2, D...  127 us
    pallas_call x1, Pallas kernels, last_rows(): pl.pallas_call(last_kernel, grid=(STEPS, U // COLUMNS), out_shape=jax.Sha...  8.26 us

profile of v6, /device:TPU:14, one launch (start us, length us, event | category | flops | bytes accessed | tf_op | source)
XLA Modules:
  0.0 135.4 jit_solution(4488325245073575736)
XLA Ops:
  0.0 127.2 %filtered.1 = bf16[3,2,4,128,1024]{4,3,2,1,0:T(8,128)(2,1)} custom-call(s32[1,3]{1,0:T(1,128)} %start_ref.1, s32[1,3]{1,0:T(1,128)} %width_ref.1, s32[4]{0:T(128)} %shift_ref.1, s32[3072]{0:T(1024)} %target_ref.1, f32[4,8,512]{2,1,0:T(8,128)} %constant.16.clone.edge_ref, bf16[4,128,2,512]{3,2,1,0:T(2,128)(2,1)} %bank_ref.1, f32[3072,256]{1,0:T(8,128)} %strain_hbm.1, ...), custom_call_target="tpu_custom_call" | custom-call | flops 12000000000 | bytes 16000000 | tf_op jit(solution)/shard_map/filtered/pallas_call | solution.py:651
  127.2 8.3 %last_rows.1 = bf16[1,1,3,256,2,1024]{5,4,3,2,1,0:T(2,128)(2,1)} custom-call(bf16[3,1024,1024]{2,1,0:T(8,128)(2,1)} %bitcast.1, bf16[512,1024]{1,0:T(8,128)(2,1)} %constant.20.clone.last_ref), custom_call_target="tpu_custom_call" | custom-call | tf_op jit(solution)/shard_map/last_rows/pallas_call | solution.py:707

commit v7 on v6

--- a/solution.py
+++ b/solution.py
@@ -484,9 +484,10 @@
     flip = jnp.where(flip, 1.0, 0.0).astype(BF16)
     packed = lax.broadcasted_iota(jnp.int32, (high, 2 * QU), 0) % SHARE + det == 0
     imag_side = lax.broadcasted_iota(jnp.int32, (high, 2 * QU), 1) >= QU
-    for o in (0, 1, 3, 2):
+    beside = 3 - 2 * (det % 2)
+    for turn, o in enumerate((0, beside, DETS - beside, 2)):
         source = (det + DETS - o) % DETS
-        if o == 0:
+        if turn == 0:
             came = turned[det]
         else:
             for d in range(DETECTORS):
@@ -499,7 +500,7 @@
         twin = jnp.concatenate([twin, twin], axis=1) * edge_ref[source][:1]
         mirrored = jnp.where(packed, twin, wide_came).astype(BF16)
         mirrored = jnp.dot(flip, mirrored, preferred_element_type=F32).astype(BF16)
-        if o == 2:
+        if turn == 3:
 
             @pl.when(upper_det)
             def _():
@@ -513,14 +514,14 @@
                 keep_low.wait()
 
         part = jnp.dot(direct, col[0, source], preferred_element_type=F32)
-        if o == 0:
+        if turn == 0:
             spec[0] = part
         else:
             spec[0] += part
-        if o == 2:
+        if turn == 3:
             gather_rows(0, psd_low, 0, 0)
         other = jnp.dot(mirrored, col[1, source], preferred_element_type=F32)
-        if o == 0:
+        if turn == 0:
             spec[1] = other
         else:
             spec[1] += other
@@ -573,11 +574,13 @@
 
     @pl.when(middle)
     def _():
-        for part in range(PARTS):
-            coherent_copy(entry, det, 0, part).wait_recv()
-            coherent_copy(entry, near, 2, part).start()
-            coherent_copy(beyond, det, 0, part).wait_recv()
-            coherent_copy(beyond, near, 3, part).start()
+        for part in range(PARTS + 1):
+            if part < PARTS:
+                coherent_copy(entry, det, 0, part).wait_recv()
+                coherent_copy(entry, near, 2, part).start()
+            if part > 0:
+                coherent_copy(beyond, det, 0, part - 1).wait_recv()
+                coherent_copy(beyond, near, 3, part - 1).start()
 
     arrive(near)
     invert(near)
@@ -695,7 +698,7 @@
     )(*operands)
 
 
-COLUMNS = 512
+COLUMNS = 1024
 
 
 def last_kernel(partial_ref, last_ref, out_ref):

time: 137 us -> 135 us (0.985)
  no operation moved by 1% of the time
where the time goes in v7:
time: 135 us; the launch traced here: 134 us
  Pallas kernels  134 us (99%)
    pallas_call x1, Pallas kernels, filtered(): pl.pallas_call(filter_kernel, out_shape=jax.ShapeDtypeStruct((STEPS, 2, D...  126 us
    pallas_call x1, Pallas kernels, last_rows(): pl.pallas_call(last_kernel, grid=(STEPS, U // COLUMNS), out_shape=jax.Sha...  7.37 us

profile of v7, /device:TPU:14, one launch (start us, length us, event | category | flops | bytes accessed | tf_op | source)
XLA Modules:
  0.0 133.8 jit_solution(13875376071399607580)
XLA Ops:
  0.0 126.5 %filtered.1 = bf16[3,2,4,128,1024]{4,3,2,1,0:T(8,128)(2,1)} custom-call(s32[1,3]{1,0:T(1,128)} %start_ref.1, s32[1,3]{1,0:T(1,128)} %width_ref.1, s32[4]{0:T(128)} %shift_ref.1, s32[3072]{0:T(1024)} %target_ref.1, f32[4,8,512]{2,1,0:T(8,128)} %constant.16.clone.edge_ref, bf16[4,128,2,512]{3,2,1,0:T(2,128)(2,1)} %bank_ref.1, f32[3072,256]{1,0:T(8,128)} %strain_hbm.1, ...), custom_call_target="tpu_custom_call" | custom-call | flops 12000000000 | bytes 16000000 | tf_op jit(solution)/shard_map/filtered/pallas_call | solution.py:654
  126.5 7.4 %last_rows.1 = bf16[1,1,3,256,2,1024]{5,4,3,2,1,0:T(2,128)(2,1)} custom-call(bf16[3,1024,1024]{2,1,0:T(8,128)(2,1)} %bitcast.1, bf16[512,1024]{1,0:T(8,128)(2,1)} %constant.20.clone.last_ref), custom_call_target="tpu_custom_call" | custom-call | tf_op jit(solution)/shard_map/last_rows/pallas_call | solution.py:710
